TPU v7x, 256 devices: a whole 4x4x8 slice. The times are simulated.
256 devices in a mesh: lon: 64 (over z, x, y_hi), lat: 4 (over y_lo, core).
Axes of the slice: x: 4, y: 4 (y_hi: 2, y_lo: 2; y = y_hi * 2 + y_lo), z: 8, core: 2. Of those that a mesh axis runs over, the one named last changes fastest.
Arguments:
- stored_blocks: bfloat16 [3, 4096, 2048], P(None, 'lon', 'lat'), may hold values from -2.5 to 2.5
- row_scale: float32 [3, 2048], P(None, 'lat'), may hold values from 0.05 to 0.5
- levels: int32 [4096, 2048], P('lon', 'lat'), may hold values from 1 to 75
- land_mask: int32 [4096, 2048], P('lon', 'lat'), may hold values 0 or 1
- cotangent: float32 [3, 4096, 2048], P(None, 'lon', 'lat'), may hold values from -6 to 6
Outputs:
- checkpoint_grad: float32 [3, 4096, 2048], P(None, 'lon', 'lat')
- scale_grad: float32 [3, 2048], P(None, 'lat')
All inputs are finite; a program needn't handle non-finite values. No bound on the sum of `land_mask` on one device may be relied on, other than what follows from the above.
Results may differ from a plain program's by a relative error of at most 0.0003.
Values sent between devices are 32-bit elements; how exact they have to be, the bound alone decides.
No kernel may reach another device: no remote copies, remote signals or barrier semaphores. Data moves between devices by JAX's collectives and lax.ppermute only.
A program may use at most 64 MiB of HBM per device.

v0:
```python
import math

import jax
import jax.numpy as jnp
from jax import lax
from jax.sharding import PartitionSpec as P

STEPS = 4


time_step = 0.5
gravity = 1.0
level_depth = 0.08
damping = 0.02
coriolis = 0.1


def with_halo(array, sides, width, wrap):
    for axis, dim in sides:
        peers, length = (lax.axis_size(axis), array.shape[dim])
        up = [(i, (i + 1) % peers) for i in range(peers if wrap else peers - 1)]
        down = [(j, i) for i, j in up]
        last = lax.slice_in_dim(array, length - width, length, axis=dim)
        leading = lax.slice_in_dim(array, 0, width, axis=dim)
        before = lax.ppermute(last, axis, up)
        after = lax.ppermute(leading, axis, down)
        array = jnp.concatenate([before, array, after], axis=dim)
    return array


def partner(value, axis, bit):
    mask = 2**bit
    pairs = [(source, source ^ mask) for source in range(lax.axis_size(axis))]
    return lax.ppermute(value, axis, pairs)


def advance(current, ocean_mask, floor_depth, spin_rows):
    height = current[0]
    east_speed = current[1]
    north_speed = current[2]
    column_depth = floor_depth + height
    flux_east = ocean_mask * column_depth * east_speed
    flux_north = ocean_mask * column_depth * north_speed
    diverge = 0.5 * (
        flux_east[2:, 1:-1] - flux_east[:-2, 1:-1] + flux_north[1:-1, 2:] - flux_north[1:-1, :-2]
    )
    surface = height[1:-1, 1:-1] - time_step * ocean_mask[1:-1, 1:-1] * diverge
    slope_east = 0.5 * (surface[2:, 1:-1] - surface[:-2, 1:-1])
    slope_north = 0.5 * (surface[1:-1, 2:] - surface[1:-1, :-2])
    ocean_inner = ocean_mask[2:-2, 2:-2]
    spin_inner = spin_rows[2:-2]
    old_east = east_speed[2:-2, 2:-2]
    old_north = north_speed[2:-2, 2:-2]
    new_east = ocean_inner * (
        (1.0 - damping) * old_east
        - time_step * gravity * slope_east
        + time_step * spin_inner * old_north
    )
    new_north = ocean_inner * (
        (1.0 - damping) * old_north
        - time_step * gravity * slope_north
        - time_step * spin_inner * old_east
    )
    return jnp.stack([surface[1:-1, 1:-1], new_east, new_north])


def spin_table(first_row, row_count, total_rows):
    row_place = first_row + jnp.arange(row_count, dtype=jnp.float32)
    return coriolis * jnp.cos(math.pi * (row_place + 0.5 - total_rows) / (2.0 * total_rows))


def lon_margin(fields, margin):
    return with_halo(fields, (("lon", 1),), margin, True)


def lat_margin(fields, margin):
    return with_halo(fields, (("lat", 2),), margin, False)


def mirror(fields):
    doublings = lax.axis_size("lon").bit_length() - 1
    for position in range(doublings):
        fields = partner(fields, "lon", position)
    return fields


def extend_block(fields, flip_signs, margin, top_flag):
    lat_cells = fields.shape[2]
    widened = lon_margin(fields, margin)
    framed = lat_margin(widened, margin)
    folded = mirror(
        jnp.flip(widened[:, :, lat_cells - margin :], axis=(1, 2)) * flip_signs[:, None, None]
    )
    north_rows = framed[:, :, lat_cells + margin :] + top_flag * folded
    return jnp.concatenate([framed[:, :, : lat_cells + margin], north_rows], axis=2)


def contract_block(framed_adj, flip_signs, margin, top_flag):
    lat_cells = framed_adj.shape[2] - 2 * margin
    lon_cells = framed_adj.shape[1] - 2 * margin
    north_adj = framed_adj[:, :, lat_cells + margin :]
    returned = mirror(jnp.flip(top_flag * north_adj, axis=(1, 2)) * flip_signs[:, None, None])
    edges = jnp.concatenate([framed_adj[:, :, :margin], north_adj], axis=2)
    edges_back = lat_margin(edges, margin)
    middle = framed_adj[:, :, margin : lat_cells + margin]
    middle = middle.at[:, :, :margin].add(edges_back[:, :, :margin])
    middle = middle.at[:, :, lat_cells - margin :].add(edges_back[:, :, 3 * margin :] + returned)
    sides = jnp.concatenate([middle[:, :margin], middle[:, lon_cells + margin :]], axis=1)
    sides_back = lon_margin(sides, margin)
    result = middle[:, margin : lon_cells + margin]
    result = result.at[:, :margin].add(sides_back[:, :margin])
    result = result.at[:, lon_cells - margin :].add(sides_back[:, 3 * margin :])
    return result


def shards(stored_blocks, row_scale, levels, land_mask, cotangent):
    batch_steps = 1
    margin = 2 * batch_steps
    lat_cells = stored_blocks.shape[2]
    top_flag = (lax.axis_index("lat") == lax.axis_size("lat") - 1).astype(jnp.float32)
    total_rows = lat_cells * lax.axis_size("lat")
    initial = stored_blocks.astype(jnp.float32) * row_scale[:, None, :]
    statics = jnp.stack([land_mask.astype(jnp.float32), level_depth * levels.astype(jnp.float32)])
    statics_ext = extend_block(statics, jnp.ones((2,), jnp.float32), margin, top_flag)
    first_row = (lax.axis_index("lat") * lat_cells - margin).astype(jnp.float32)
    spin_ext = spin_table(first_row, lat_cells + 2 * margin, total_rows)
    state_signs = jnp.array([1.0, -1.0, -1.0], jnp.float32)

    def run_batch(framed):
        framed = advance(framed, statics_ext[0], statics_ext[1], spin_ext)
        return framed

    pullbacks = []
    current = initial
    for segment in range(STEPS // batch_steps):
        framed = extend_block(current, state_signs, margin, top_flag)
        current, pullback = jax.vjp(run_batch, framed)
        pullbacks.append(pullback)
    adjoint = cotangent
    for pullback in reversed(pullbacks):
        framed_adj = pullback(adjoint)[0]
        adjoint = contract_block(framed_adj, state_signs, margin, top_flag)
    checkpoint_grad = adjoint * row_scale[:, None, :]
    partial_rows = jnp.sum(adjoint * stored_blocks.astype(jnp.float32), axis=1)
    scale_grad = lax.psum(partial_rows, "lon")
    return (checkpoint_grad, scale_grad)


def solution(mesh):
    return jax.shard_map(
        shards,
        mesh=mesh,
        in_specs=(
            P(None, "lon", "lat"),
            P(None, "lat"),
            P("lon", "lat"),
            P("lon", "lat"),
            P(None, "lon", "lat"),
        ),
        out_specs=(P(None, "lon", "lat"), P(None, "lat")),
        check_vma=False,
    )
```

profile of v0, /device:TPU:8, one launch (start us, length us, event | category | flops | bytes accessed | tf_op | source)
XLA Modules:
  0.0 632.0 jit_solution(9136362305001121331)
XLA Ops:
  4.0 7.6 %collective-permute-start.1 = (f32[2,2,512]{2,1,0:T(2,128)S(1)}, f32[2,2,512]{2,1,0:T(2,128)S(1)}, u32[]{:S(2)}, u32[]{:S(2)}) collective-permute-start(f32[2,2,512]{2,1,0:T(2,128)S(1)} %get-tuple-element.287), channel_id=1, source_target_pairs={{4,0},{8,4},{12,8},{16,12},{20,16},{24,20},{28,24},{32,28},{36,32}... | collective-permute-start | bytes 24584 | tf_op jit(solution)/shard_map/ppermute | solution.py:26
  11.8 7.7 %collective-permute-start.11 = (f32[3,2,512]{2,1,0:T(2,128)S(1)}, f32[3,2,512]{2,1,0:T(2,128)S(1)}, u32[]{:S(2)}, u32[]{:S(2)}) collective-permute-start(f32[3,2,512]{2,1,0:T(2,128)S(1)} %get-tuple-element.280), channel_id=1, source_target_pairs={{4,0},{8,4},{12,8},{16,12},{20,16},{24,20},{28,24},{32,28},{36,32}... | collective-permute-start | bytes 36872 | tf_op jit(solution)/shard_map/ppermute | solution.py:26
  64.4 6.9 %collective-permute-done.18 = f32[3,68,2]{2,1,0:T(8,128)S(1)} collective-permute-done((f32[3,68,2]{2,1,0:T(8,128)S(1)}, f32[3,68,2]{2,1,0:T(8,128)S(1)}, u32[]{:S(2)}, u32[]{:S(2)}) %collective-permute-start.18) | collective-permute-done | bytes 1664 | tf_op jit(solution)/shard_map/ppermute | solution.py:34
  71.4 8.6 %collective-permute-done.19 = f32[3,68,2]{2,1,0:T(8,128)S(1)} collective-permute-done((f32[3,68,2]{2,1,0:T(8,128)S(1)}, f32[3,68,2]{2,1,0:T(8,128)S(1)}, u32[]{:S(2)}, u32[]{:S(2)}) %collective-permute-start.19) | collective-permute-done | bytes 1664 | tf_op jit(solution)/shard_map/ppermute | solution.py:34
  83.0 7.0 %collective-permute-start.21 = (f32[3,2,512]{2,1,0:T(2,128)S(1)}, f32[3,2,512]{2,1,0:T(2,128)S(1)}, u32[]{:S(2)}, u32[]{:S(2)}) collective-permute-start(f32[3,2,512]{2,1,0:T(2,128)S(1)} %get-tuple-element.278), channel_id=1, source_target_pairs={{4,0},{8,4},{12,8},{16,12},{20,16},{24,20},{28,24},{32,28},{36,32}... | collective-permute-start | bytes 36872 | tf_op jit(solution)/shard_map/ppermute | solution.py:26
  92.3 6.2 collective-permute-done.24
  123.2 7.2 %collective-permute-done.29 = f32[3,68,2]{2,1,0:T(8,128)S(1)} collective-permute-done((f32[3,68,2]{2,1,0:T(8,128)S(1)}, f32[3,68,2]{2,1,0:T(8,128)S(1)}, u32[]{:S(2)}, u32[]{:S(2)}) %collective-permute-start.29) | collective-permute-done | bytes 1664 | tf_op jit(solution)/shard_map/ppermute | solution.py:34
  133.0 8.0 %collective-permute-start.31 = (f32[3,2,512]{2,1,0:T(2,128)S(1)}, f32[3,2,512]{2,1,0:T(2,128)S(1)}, u32[]{:S(2)}, u32[]{:S(2)}) collective-permute-start(f32[3,2,512]{2,1,0:T(2,128)S(1)} %get-tuple-element.276), channel_id=1, source_target_pairs={{4,0},{8,4},{12,8},{16,12},{20,16},{24,20},{28,24},{32,28},{36,32}... | collective-permute-start | bytes 36872 | tf_op jit(solution)/shard_map/ppermute | solution.py:26
  143.3 6.2 collective-permute-done.34
  154.3 6.2 collective-permute-done.36
  185.7 6.6 %collective-permute-start.41 = (f32[3,2,512]{2,1,0:T(2,128)S(1)}, f32[3,2,512]{2,1,0:T(2,128)S(1)}, u32[]{:S(2)}, u32[]{:S(2)}) collective-permute-start(f32[3,2,512]{2,1,0:T(2,128)S(1)} %get-tuple-element.274), channel_id=1, source_target_pairs={{4,0},{8,4},{12,8},{16,12},{20,16},{24,20},{28,24},{32,28},{36,32}... | collective-permute-start | bytes 36872 | tf_op jit(solution)/shard_map/ppermute | solution.py:26
  238.2 6.2 collective-permute-done.52
  250.3 6.2 collective-permute-done.54
  270.5 8.2 %collective-permute-done.57 = f32[3,68,2]{2,1,0:T(8,128)} collective-permute-done((f32[3,68,2]{2,1,0:T(8,128)}, f32[3,68,2]{2,1,0:T(8,128)}, u32[]{:S(2)}, u32[]{:S(2)}) %collective-permute-start.57) | collective-permute-done | bytes 1664 | tf_op jit(solution)/shard_map/ppermute | solution.py:34
  281.0 7.8 %collective-permute-start.59 = (f32[3,2,512]{2,1,0:T(2,128)S(1)}, f32[3,2,512]{2,1,0:T(2,128)S(1)}, u32[]{:S(2)}, u32[]{:S(2)}) collective-permute-start(f32[3,2,512]{2,1,0:T(2,128)S(1)} %get-tuple-element.261), channel_id=1, source_target_pairs={{4,0},{8,4},{12,8},{16,12},{20,16},{24,20},{28,24},{32,28},{36,32}... | collective-permute-start | bytes 36872 | tf_op jit(solution)/shard_map/ppermute | solution.py:26
  292.4 6.2 collective-permute-done.62
  303.4 6.2 collective-permute-done.64
  323.8 7.0 %collective-permute-done.67 = f32[3,68,2]{2,1,0:T(8,128)S(1)} collective-permute-done((f32[3,68,2]{2,1,0:T(8,128)S(1)}, f32[3,68,2]{2,1,0:T(8,128)S(1)}, u32[]{:S(2)}, u32[]{:S(2)}) %collective-permute-start.67) | collective-permute-done | bytes 1664 | tf_op jit(solution)/shard_map/ppermute | solution.py:34
  332.0 7.8 %collective-permute-start.69 = (f32[3,2,512]{2,1,0:T(2,128)S(1)}, f32[3,2,512]{2,1,0:T(2,128)S(1)}, u32[]{:S(2)}, u32[]{:S(2)}) collective-permute-start(f32[3,2,512]{2,1,0:T(2,128)S(1)} %get-tuple-element.259), channel_id=1, source_target_pairs={{4,0},{8,4},{12,8},{16,12},{20,16},{24,20},{28,24},{32,28},{36,32}... | collective-permute-start | bytes 36872 | tf_op jit(solution)/shard_map/ppermute | solution.py:26
  375.9 6.5 %collective-permute-done.77 = f32[3,68,2]{2,1,0:T(8,128)S(1)} collective-permute-done((f32[3,68,2]{2,1,0:T(8,128)S(1)}, f32[3,68,2]{2,1,0:T(8,128)S(1)}, u32[]{:S(2)}, u32[]{:S(2)}) %collective-permute-start.77) | collective-permute-done | bytes 1664 | tf_op jit(solution)/shard_map/ppermute | solution.py:34
  383.7 7.9 %collective-permute-start.79 = (f32[3,2,512]{2,1,0:T(2,128)S(1)}, f32[3,2,512]{2,1,0:T(2,128)S(1)}, u32[]{:S(2)}, u32[]{:S(2)}) collective-permute-start(f32[3,2,512]{2,1,0:T(2,128)S(1)} %get-tuple-element.257), channel_id=1, source_target_pairs={{4,0},{8,4},{12,8},{16,12},{20,16},{24,20},{28,24},{32,28},{36,32}... | collective-permute-start | bytes 36872 | tf_op jit(solution)/shard_map/ppermute | solution.py:26
  426.8 6.5 %collective-permute-done.87 = f32[3,68,2]{2,1,0:T(8,128)S(1)} collective-permute-done((f32[3,68,2]{2,1,0:T(8,128)S(1)}, f32[3,68,2]{2,1,0:T(8,128)S(1)}, u32[]{:S(2)}, u32[]{:S(2)}) %collective-permute-start.87) | collective-permute-done | bytes 1664 | tf_op jit(solution)/shard_map/ppermute | solution.py:34
  434.5 7.7 %collective-permute-start.89 = (f32[3,2,512]{2,1,0:T(2,128)S(1)}, f32[3,2,512]{2,1,0:T(2,128)S(1)}, u32[]{:S(2)}, u32[]{:S(2)}) collective-permute-start(f32[3,2,512]{2,1,0:T(2,128)S(1)} %get-tuple-element.255), channel_id=1, source_target_pairs={{4,0},{8,4},{12,8},{16,12},{20,16},{24,20},{28,24},{32,28},{36,32}... | collective-permute-start | bytes 36872 | tf_op jit(solution)/shard_map/ppermute | solution.py:26
  444.7 186.9 %psum.7 = f32[3,512]{1,0:T(4,128)} all-reduce(f32[3,512]{1,0:T(4,128)S(1)} %get-tuple-element.271), channel_id=1, replica_groups=mesh['lon'=64,'lat'=4] {'lon'}, use_global_device_ids=true, to_apply=%region_1.2 | all-reduce | flops 1536 | bytes 12288 | tf_op jit(solution)/shard_map/psum | solution.py:145
  (305 shorter events, 280.0 us)
Async XLA Ops:
  1.7 17.8 %collective-permute-start = (f32[2,2,512]{2,1,0:T(2,128)S(1)}, f32[2,2,512]{2,1,0:T(2,128)S(1)}, u32[]{:S(2)}, u32[]{:S(2)}) collective-permute-start(f32[2,2,512]{2,1,0:T(2,128)S(1)} %get-tuple-element.286), channel_id=1, source_target_pairs={{0,4},{4,8},{8,12},{12,16},{16,20},{20,24},{24,28},{28,32},{32,36}... | collective-permute-start | bytes 24584 | tf_op jit(solution)/shard_map/ppermute | solution.py:25
  4.0 15.5 %collective-permute-start.1 = (f32[2,2,512]{2,1,0:T(2,128)S(1)}, f32[2,2,512]{2,1,0:T(2,128)S(1)}, u32[]{:S(2)}, u32[]{:S(2)}) collective-permute-start(f32[2,2,512]{2,1,0:T(2,128)S(1)} %get-tuple-element.287), channel_id=1, source_target_pairs={{4,0},{8,4},{12,8},{16,12},{20,16},{24,20},{28,24},{32,28},{36,32}... | collective-permute-start | bytes 24584 | tf_op jit(solution)/shard_map/ppermute | solution.py:26
  11.7 18.5 %collective-permute-start.10 = (f32[3,2,512]{2,1,0:T(2,128)S(1)}, f32[3,2,512]{2,1,0:T(2,128)S(1)}, u32[]{:S(2)}, u32[]{:S(2)}) collective-permute-start(f32[3,2,512]{2,1,0:T(2,128)S(1)} %get-tuple-element.279), channel_id=1, source_target_pairs={{0,4},{4,8},{8,12},{12,16},{16,20},{20,24},{24,28},{28,32},{32,36}... | collective-permute-start | bytes 36872 | tf_op jit(solution)/shard_map/ppermute | solution.py:25
  11.8 18.4 %collective-permute-start.11 = (f32[3,2,512]{2,1,0:T(2,128)S(1)}, f32[3,2,512]{2,1,0:T(2,128)S(1)}, u32[]{:S(2)}, u32[]{:S(2)}) collective-permute-start(f32[3,2,512]{2,1,0:T(2,128)S(1)} %get-tuple-element.280), channel_id=1, source_target_pairs={{4,0},{8,4},{12,8},{16,12},{20,16},{24,20},{28,24},{32,28},{36,32}... | collective-permute-start | bytes 36872 | tf_op jit(solution)/shard_map/ppermute | solution.py:26
  40.4 10.5 %collective-permute-start.15 = (f32[3,68,2]{2,1,0:T(8,128)S(1)}, f32[3,68,2]{2,1,0:T(8,128)S(1)}, u32[]{:S(2)}, u32[]{:S(2)}) collective-permute-start(f32[3,68,2]{2,1,0:T(8,128)S(1)} %collective-permute-done.14), channel_id=1, source_target_pairs={{0,8},{4,12},{8,0},{12,4},{16,24},{20,28},{24,16},{28,20},{32,40},... | collective-permute-start | bytes 4904 | tf_op jit(solution)/shard_map/ppermute | solution.py:34
  41.0 14.4 %collective-permute-start.3 = (f32[2,68,2]{2,1,0:T(8,128)S(1)}, f32[2,68,2]{2,1,0:T(8,128)S(1)}, u32[]{:S(2)}, u32[]{:S(2)}) collective-permute-start(f32[2,68,2]{2,1,0:T(8,128)S(1)} %get-tuple-element.285), channel_id=1, source_target_pairs={{1,0},{2,1},{3,2},{5,4},{6,5},{7,6},{9,8},{10,9},{11,10},{13,12},{... | collective-permute-start | bytes 3272 | tf_op jit(solution)/shard_map/ppermute | solution.py:26
  45.9 13.3 %collective-permute-start.9 = (f32[2,68,2]{2,1,0:T(8,128)S(1)}, f32[2,68,2]{2,1,0:T(8,128)S(1)}, u32[]{:S(2)}, u32[]{:S(2)}) collective-permute-start(f32[2,68,2]{2,1,0:T(8,128)S(1)} %collective-permute-done.8), channel_id=1, source_target_pairs={{0,128},{4,132},{8,136},{12,140},{16,144},{20,148},{24,152},{28,15... | collective-permute-start | bytes 3272 | tf_op jit(solution)/shard_map/ppermute | solution.py:34
  51.5 12.7 %collective-permute-start.2 = (f32[2,68,2]{2,1,0:T(8,128)S(1)}, f32[2,68,2]{2,1,0:T(8,128)S(1)}, u32[]{:S(2)}, u32[]{:S(2)}) collective-permute-start(f32[2,68,2]{2,1,0:T(8,128)S(1)} %get-tuple-element.284), channel_id=1, source_target_pairs={{0,1},{1,2},{2,3},{4,5},{5,6},{6,7},{8,9},{9,10},{10,11},{12,13},{... | collective-permute-start | bytes 3272 | tf_op jit(solution)/shard_map/ppermute | solution.py:25
  53.5 26.6 %collective-permute-start.12 = (f32[3,68,2]{2,1,0:T(8,128)S(1)}, f32[3,68,2]{2,1,0:T(8,128)S(1)}, u32[]{:S(2)}, u32[]{:S(2)}) collective-permute-start(f32[3,68,2]{2,1,0:T(8,128)S(1)} %get-tuple-element.269), channel_id=1, source_target_pairs={{0,1},{1,2},{2,3},{4,5},{5,6},{6,7},{8,9},{9,10},{10,11},{12,13},{... | collective-permute-start | bytes 4904 | tf_op jit(solution)/shard_map/ppermute | solution.py:25
  55.4 16.0 %collective-permute-start.13 = (f32[3,68,2]{2,1,0:T(8,128)S(1)}, f32[3,68,2]{2,1,0:T(8,128)S(1)}, u32[]{:S(2)}, u32[]{:S(2)}) collective-permute-start(f32[3,68,2]{2,1,0:T(8,128)S(1)} %get-tuple-element.270), channel_id=1, source_target_pairs={{1,0},{2,1},{3,2},{5,4},{6,5},{7,6},{9,8},{10,9},{11,10},{13,12},{... | collective-permute-start | bytes 4904 | tf_op jit(solution)/shard_map/ppermute | solution.py:26
  81.8 9.8 %collective-permute-start.20 = (f32[3,2,512]{2,1,0:T(2,128)S(1)}, f32[3,2,512]{2,1,0:T(2,128)S(1)}, u32[]{:S(2)}, u32[]{:S(2)}) collective-permute-start(f32[3,2,512]{2,1,0:T(2,128)S(1)} %get-tuple-element.277), channel_id=1, source_target_pairs={{0,4},{4,8},{8,12},{12,16},{16,20},{20,24},{24,28},{28,32},{32,36}... | collective-permute-start | bytes 36872 | tf_op jit(solution)/shard_map/ppermute | solution.py:25
  166.4 11.0 %collective-permute-start.33 = (f32[3,68,2]{2,1,0:T(8,128)S(1)}, f32[3,68,2]{2,1,0:T(8,128)S(1)}, u32[]{:S(2)}, u32[]{:S(2)}) collective-permute-start(f32[3,68,2]{2,1,0:T(8,128)S(1)} %get-tuple-element.266), channel_id=1, source_target_pairs={{1,0},{2,1},{3,2},{5,4},{6,5},{7,6},{9,8},{10,9},{11,10},{13,12},{... | collective-permute-start | bytes 4904 | tf_op jit(solution)/shard_map/ppermute | solution.py:26
  171.8 10.6 %collective-permute-start.39 = (f32[3,68,2]{2,1,0:T(8,128)S(1)}, f32[3,68,2]{2,1,0:T(8,128)S(1)}, u32[]{:S(2)}, u32[]{:S(2)}) collective-permute-start(f32[3,68,2]{2,1,0:T(8,128)S(1)} %collective-permute-done.38), channel_id=1, source_target_pairs={{0,128},{4,132},{8,136},{12,140},{16,144},{20,148},{24,152},{28,15... | collective-permute-start | bytes 4904 | tf_op jit(solution)/shard_map/ppermute | solution.py:34
  218.6 10.7 %collective-permute-start.43 = (f32[3,68,2]{2,1,0:T(8,128)S(1)}, f32[3,68,2]{2,1,0:T(8,128)S(1)}, u32[]{:S(2)}, u32[]{:S(2)}) collective-permute-start(f32[3,68,2]{2,1,0:T(8,128)S(1)} %copy-done.10), channel_id=1, source_target_pairs={{1,0},{2,1},{3,2},{5,4},{6,5},{7,6},{9,8},{10,9},{11,10},{13,12},{... | collective-permute-start | bytes 4904 | tf_op jit(solution)/shard_map/ppermute | solution.py:26
  224.8 10.0 %collective-permute-start.49 = (f32[3,68,2]{2,1,0:T(8,128)S(1)}, f32[3,68,2]{2,1,0:T(8,128)S(1)}, u32[]{:S(2)}, u32[]{:S(2)}) collective-permute-start(f32[3,68,2]{2,1,0:T(8,128)S(1)} %collective-permute-done.48), channel_id=1, source_target_pairs={{0,128},{4,132},{8,136},{12,140},{16,144},{20,148},{24,152},{28,15... | collective-permute-start | bytes 4904 | tf_op jit(solution)/shard_map/ppermute | solution.py:34
  256.6 13.3 %collective-permute-start.50 = (f32[3,68,2]{2,1,0:T(8,128)S(1)}, f32[3,68,2]{2,1,0:T(8,128)S(1)}, u32[]{:S(2)}, u32[]{:S(2)}) collective-permute-start(f32[3,68,2]{2,1,0:T(8,128)S(1)} %get-tuple-element.245), channel_id=1, source_target_pairs={{0,1},{1,2},{2,3},{4,5},{5,6},{6,7},{8,9},{9,10},{10,11},{12,13},{... | collective-permute-start | bytes 4904 | tf_op jit(solution)/shard_map/ppermute | solution.py:25
  267.7 11.1 %collective-permute-start.57 = (f32[3,68,2]{2,1,0:T(8,128)}, f32[3,68,2]{2,1,0:T(8,128)}, u32[]{:S(2)}, u32[]{:S(2)}) collective-permute-start(f32[3,68,2]{2,1,0:T(8,128)} %collective-permute-done.56), channel_id=1, source_target_pairs={{0,128},{4,132},{8,136},{12,140},{16,144},{20,148},{24,152},{28,15... | collective-permute-start | bytes 4904 | tf_op jit(solution)/shard_map/ppermute | solution.py:34
  309.6 13.4 %collective-permute-start.60 = (f32[3,68,2]{2,1,0:T(8,128)S(1)}, f32[3,68,2]{2,1,0:T(8,128)S(1)}, u32[]{:S(2)}, u32[]{:S(2)}) collective-permute-start(f32[3,68,2]{2,1,0:T(8,128)S(1)} %get-tuple-element.241), channel_id=1, source_target_pairs={{0,1},{1,2},{2,3},{4,5},{5,6},{6,7},{8,9},{9,10},{10,11},{12,13},{... | collective-permute-start | bytes 4904 | tf_op jit(solution)/shard_map/ppermute | solution.py:25
  320.7 10.2 %collective-permute-start.67 = (f32[3,68,2]{2,1,0:T(8,128)S(1)}, f32[3,68,2]{2,1,0:T(8,128)S(1)}, u32[]{:S(2)}, u32[]{:S(2)}) collective-permute-start(f32[3,68,2]{2,1,0:T(8,128)S(1)} %collective-permute-done.66), channel_id=1, source_target_pairs={{0,128},{4,132},{8,136},{12,140},{16,144},{20,148},{24,152},{28,15... | collective-permute-start | bytes 4904 | tf_op jit(solution)/shard_map/ppermute | solution.py:34
  360.8 14.5 %collective-permute-start.70 = (f32[3,68,2]{2,1,0:T(8,128)S(1)}, f32[3,68,2]{2,1,0:T(8,128)S(1)}, u32[]{:S(2)}, u32[]{:S(2)}) collective-permute-start(f32[3,68,2]{2,1,0:T(8,128)S(1)} %get-tuple-element.237), channel_id=1, source_target_pairs={{0,1},{1,2},{2,3},{4,5},{5,6},{6,7},{8,9},{9,10},{10,11},{12,13},{... | collective-permute-start | bytes 4904 | tf_op jit(solution)/shard_map/ppermute | solution.py:25
  366.1 9.8 %collective-permute-start.71 = (f32[3,68,2]{2,1,0:T(8,128)S(1)}, f32[3,68,2]{2,1,0:T(8,128)S(1)}, u32[]{:S(2)}, u32[]{:S(2)}) collective-permute-start(f32[3,68,2]{2,1,0:T(8,128)S(1)} %get-tuple-element.236), channel_id=1, source_target_pairs={{1,0},{2,1},{3,2},{5,4},{6,5},{7,6},{9,8},{10,9},{11,10},{13,12},{... | collective-permute-start | bytes 4904 | tf_op jit(solution)/shard_map/ppermute | solution.py:26
  371.8 10.7 %collective-permute-start.77 = (f32[3,68,2]{2,1,0:T(8,128)S(1)}, f32[3,68,2]{2,1,0:T(8,128)S(1)}, u32[]{:S(2)}, u32[]{:S(2)}) collective-permute-start(f32[3,68,2]{2,1,0:T(8,128)S(1)} %collective-permute-done.76), channel_id=1, source_target_pairs={{0,128},{4,132},{8,136},{12,140},{16,144},{20,148},{24,152},{28,15... | collective-permute-start | bytes 4904 | tf_op jit(solution)/shard_map/ppermute | solution.py:34
  412.0 14.1 %collective-permute-start.80 = (f32[3,68,2]{2,1,0:T(8,128)S(1)}, f32[3,68,2]{2,1,0:T(8,128)S(1)}, u32[]{:S(2)}, u32[]{:S(2)}) collective-permute-start(f32[3,68,2]{2,1,0:T(8,128)S(1)} %get-tuple-element.233), channel_id=1, source_target_pairs={{0,1},{1,2},{2,3},{4,5},{5,6},{6,7},{8,9},{9,10},{10,11},{12,13},{... | collective-permute-start | bytes 4904 | tf_op jit(solution)/shard_map/ppermute | solution.py:25
  423.1 10.2 %collective-permute-start.87 = (f32[3,68,2]{2,1,0:T(8,128)S(1)}, f32[3,68,2]{2,1,0:T(8,128)S(1)}, u32[]{:S(2)}, u32[]{:S(2)}) collective-permute-start(f32[3,68,2]{2,1,0:T(8,128)S(1)} %collective-permute-done.86), channel_id=1, source_target_pairs={{0,128},{4,132},{8,136},{12,140},{16,144},{20,148},{24,152},{28,15... | collective-permute-start | bytes 4904 | tf_op jit(solution)/shard_map/ppermute | solution.py:34
  (79 other events, 515.7 us)
where the time goes:
time: 642 us; the launch traced here: 632 us
  waiting for transfers between devices  270 us (42%)
  blocking collectives  187 us (29%)
  starting transfers between devices  142 us (22%)
  local copies, waits for them, and re-layouts  15.9 us (2%)
  other arithmetic  15.1 us (2%)
    ppermute x54, waiting for transfers between devices, partner(): return lax.ppermute(value, axis, pairs)  259 us
    psum x1, blocking collectives, shards(): scale_grad = lax.psum(partial_rows, 'lon')  187 us
    ppermute x18, starting transfers between devices, with_halo(): after = lax.ppermute(leading, axis, down)  89.7 us
    ppermute x54, starting transfers between devices, partner(): return lax.ppermute(value, axis, pairs)  29.2 us
    ppermute x18, starting transfers between devices, with_halo(): before = lax.ppermute(last, axis, up)  23.2 us
  transfers between devices with their start and end apart: 90, of which 57 were waited for; matrix products, arithmetic and copies ran while one was open for 1% of the time, Pallas kernels for 0%

commit v1 on v0

v1 whole, which is shorter than its diff:
```python
import math

import jax
import jax.numpy as jnp
from jax import lax
from jax.experimental import pallas as pl
from jax.experimental.pallas import tpu as pltpu
from jax.sharding import PartitionSpec as P

STEPS = 4
GRAVITY = 1.0
TIME_STEP = 0.5
LEVEL_DEPTH = 0.08
KEEP = 1.0 - 0.02
CORIOLIS = 0.1
HALF = 0.5 * TIME_STEP

COLS = 64
ROWS = 512
LANES = 128
TILES = ROWS // LANES
WIDE = 12
THIN = 8
BASE = 24
HEIGHT = 112
PACK = 88

WIDTHS = (WIDE,) * 5 + (THIN,) * 3
PLACES = tuple(sum(WIDTHS[:f]) for f in range(8))
SIGNS = (1.0, 1.0, 1.0, -1.0, -1.0, 1.0, -1.0, -1.0)


def lanes_of(shape):
    return lax.broadcasted_iota(jnp.int32, shape, len(shape) - 1)


def own_fields(stored, scale, levels, mask, cot):
    ocean = mask.astype(jnp.float32)
    floor = ocean * (LEVEL_DEPTH * levels.astype(jnp.float32))
    state = [stored[k].astype(jnp.float32) * scale[k : k + 1] for k in range(3)]
    return [ocean, floor] + state + [cot[0], ocean * cot[1], ocean * cot[2]]


def lon_pack_kernel(
    st_lo, st_hi, scale, lev_lo, lev_hi, mask_lo, mask_hi, cot_lo, cot_hi, a_ref, b_ref
):
    odd = lax.rem(lax.axis_index("lon"), 2) == 1
    low = own_fields(st_lo[...], scale[...], lev_lo[...], mask_lo[...], cot_lo[...])
    high = own_fields(st_hi[...], scale[...], lev_hi[...], mask_hi[...], cot_hi[...])
    for f in range(8):
        width, place = WIDTHS[f], PLACES[f]
        lower, upper = low[f][:width], high[f][16 - width :]
        a_ref[place : place + width] = jnp.where(odd, lower, upper)
        b_ref[place : place + width] = jnp.where(odd, upper, lower)
    a_ref[84:88] = jnp.zeros((4, ROWS), jnp.float32)
    b_ref[84:88] = jnp.zeros((4, ROWS), jnp.float32)


def lon_pack(stored, scale, levels, mask, cot):
    last = COLS // 16 - 1
    three = [pl.BlockSpec((3, 16, ROWS), lambda _, b=b: (0, b, 0)) for b in (0, last)]
    one = [pl.BlockSpec((16, ROWS), lambda _, b=b: (b, 0)) for b in (0, last)]
    out = jax.ShapeDtypeStruct((PACK, ROWS), jnp.float32)
    return pl.pallas_call(
        lon_pack_kernel,
        grid=(1,),
        in_specs=[*three, pl.BlockSpec((3, ROWS), lambda _: (0, 0)), *one, *one, *three],
        out_specs=[pl.BlockSpec((PACK, ROWS), lambda _: (0, 0))] * 2,
        out_shape=[out, out],
        name="lon_pack",
    )(stored, stored, scale, levels, levels, mask, mask, cot, cot)


def lat_pack_kernel(
    st_s, st_n, sc_s, sc_n, lev_s, lev_n, mask_s, mask_n, cot_s, cot_n, a_s, a_n, b_s, b_n,
    out_a, out_b, south, north,
):
    odd = lax.rem(lax.axis_index("lon"), 2) == 1
    lat = lax.axis_index("lat")
    upper = lax.rem(lat, 2) == 1
    top = lat == lax.axis_size("lat") - 1

    def pack(fields, to_south):
        total = jnp.zeros((fields[0].shape[0], LANES), jnp.float32)
        lane = lanes_of(total.shape)
        for f in range(8):
            width, place = WIDTHS[f], PLACES[f]
            shift = place if to_south else (place + width) % LANES
            moved = fields[f] if shift == 0 else pltpu.roll(fields[f], shift, 1)
            total = jnp.where((lane >= place) & (lane < place + width), moved, total)
        return total

    for dst, st, sc, lev, mask, cot, a, b, to_south in (
        (south, st_s, sc_s, lev_s, mask_s, cot_s, a_s, b_s, True),
        (north, st_n, sc_n, lev_n, mask_n, cot_n, a_n, b_n, False),
    ):
        dst[WIDE : WIDE + COLS] = pack(
            own_fields(st[...], sc[...], lev[...], mask[...], cot[...]), to_south
        )
        for side in range(2):
            fields = []
            for f in range(8):
                rows = pl.ds(PLACES[f], WIDTHS[f])
                piece = jnp.where(odd == (side == 0), a[rows], b[rows])
                if WIDTHS[f] < WIDE:
                    gap = jnp.zeros((WIDE - WIDTHS[f], LANES), jnp.float32)
                    piece = jnp.concatenate([gap, piece] if side == 0 else [piece, gap], axis=0)
                fields.append(piece)
            start = 0 if side == 0 else WIDE + COLS
            dst[start : start + WIDE] = pack(fields, to_south)
    out_a[...] = jnp.where(upper, south[...], north[...])
    out_b[...] = jnp.where(upper, north[...], south[...])

    @pl.when(top)
    def _():
        i = lax.broadcasted_iota(jnp.int32, (PACK, PACK), 0)
        j = lax.broadcasted_iota(jnp.int32, (PACK, PACK), 1)
        flip_cols = jnp.where(i + j == PACK - 1, 1.0, 0.0)
        i = lax.broadcasted_iota(jnp.int32, (LANES, LANES), 0)
        j = lax.broadcasted_iota(jnp.int32, (LANES, LANES), 1)
        flip_rows = jnp.zeros((LANES, LANES), jnp.float32)
        for f in range(8):
            first, last = PLACES[f], PLACES[f] + WIDTHS[f] - 1
            here = (i >= first) & (i <= last) & (i + j == first + last)
            flip_rows = jnp.where(here, SIGNS[f], flip_rows)
        exact = dict(precision=lax.Precision.HIGHEST, preferred_element_type=jnp.float32)
        out_b[...] = jnp.dot(flip_cols, jnp.dot(north[...], flip_rows, **exact), **exact)


def lat_pack(stored, scale, levels, mask, cot, from_a, from_b):
    ends = (0, TILES - 1)
    three = [pl.BlockSpec((3, COLS, LANES), lambda _, b=b: (0, 0, b)) for b in ends]
    scales = [pl.BlockSpec((3, LANES), lambda _, b=b: (0, b)) for b in ends]
    one = [pl.BlockSpec((COLS, LANES), lambda _, b=b: (0, b)) for b in ends]
    margin = [pl.BlockSpec((PACK, LANES), lambda _, b=b: (0, b)) for b in ends]
    out = jax.ShapeDtypeStruct((PACK, LANES), jnp.float32)
    return pl.pallas_call(
        lat_pack_kernel,
        grid=(1,),
        in_specs=[*three, *scales, *one, *one, *three, *margin, *margin],
        out_specs=[pl.BlockSpec((PACK, LANES), lambda _: (0, 0))] * 2,
        out_shape=[out, out],
        scratch_shapes=[pltpu.VMEM((PACK, LANES), jnp.float32)] * 2,
        name="lat_pack",
    )(
        stored, stored, scale, scale, levels, levels, mask, mask, cot, cot,
        from_a, from_a, from_b, from_b,
    )


def main_kernel(
    stored, scale, levels, mask, cot, spin, lon_a, lon_b, lat_a, lat_b,
    grad, partial,
    m, m0, u0, u1, u2, u3, v0, v1, v2, v3, w0, w1, w2, w3, ea, eb, fe, q, la, lb, le,
):
    odd = lax.rem(lax.axis_index("lon"), 2) == 1
    upper = lax.rem(lax.axis_index("lat"), 2) == 1
    us, vs, ws = (u0, u1, u2, u3), (v0, v1, v2, v3), (w0, w1, w2, w3)
    fields = (m, m0, ea, u0, v0, le, la, lb)
    every = TILES + 1

    for f in range(8):
        for row in (slice(0, 16), slice(96, HEIGHT)):
            fields[f][:, row] = jnp.zeros((every, 16, LANES), jnp.float32)
        fields[f][TILES, 16:96] = jnp.zeros((80, LANES), jnp.float32)
    for t in range(TILES):
        at = slice(t * LANES, (t + 1) * LANES)
        own = own_fields(
            stored[:, :, at], scale[:, at], levels[:, at], mask[:, at], cot[:, :, at]
        )
        for f in range(8):
            fields[f][t, BASE : BASE + COLS] = own[f]
            width, rows = WIDTHS[f], slice(PLACES[f], PLACES[f] + WIDTHS[f])
            from_a, from_b = lon_a[rows, at], lon_b[rows, at]
            fields[f][t, BASE - width : BASE] = jnp.where(odd, from_a, from_b)
            fields[f][t, BASE + COLS : BASE + COLS + width] = jnp.where(odd, from_b, from_a)
    north = jnp.where(upper, lat_b[...], lat_a[...])
    south = jnp.where(upper, lat_a[...], lat_b[...])
    lane = lanes_of((PACK, LANES))
    for f in range(8):
        width, place = WIDTHS[f], PLACES[f]
        up = pltpu.roll(north, (LANES - place) % LANES, 1) if place else north
        down = pltpu.roll(south, LANES - width - place, 1)
        edge = jnp.where(lane < width, up, jnp.where(lane >= LANES - width, down, 0.0))
        fields[f][TILES, BASE - WIDE : BASE + COLS + WIDE] = edge

    first = lanes_of((every, 8, LANES)) == 0
    final = lanes_of((every, 8, LANES)) == LANES - 1

    def lat_diff(x):
        ahead = pltpu.roll(x, LANES - 1, 2)
        behind = pltpu.roll(x, 1, 2)
        ahead = jnp.where(final, jnp.concatenate([ahead[1:], ahead[:1]], axis=0), ahead)
        behind = jnp.where(first, jnp.concatenate([behind[-1:], behind[:-1]], axis=0), behind)
        return ahead - behind

    def lon_diff(ref, r):
        return ref[:, pl.ds(r + 1, 8)] - ref[:, pl.ds(r - 1, 8)]

    def sweep(start, stop, body):
        for r in range(start, stop, 8):
            body(r, pl.ds(r, 8))

    turn = spin[...]

    def start_step(r, here):
        w = m0[:, here] + m[:, here] * ea[:, here]
        w0[:, here] = w
        fe[:, here] = w * u0[:, here]

    sweep(8, 104, start_step)

    for k in range(STEPS - 1):
        e, s = (ea, eb) if k % 2 == 0 else (eb, ea)
        u, v, w, u_next, v_next, w_next = us[k], vs[k], ws[k], us[k + 1], vs[k + 1], ws[k + 1]
        lo, hi = ((8, 104), (8, 104), (16, 96))[k]
        lo_s, hi_s = ((8, 104), (8, 104), (16, 96))[k]
        if k == 1:
            lo, hi = 16, 96

        def height_pass(r, here):
            diverge = lon_diff(fe, r) + lat_diff(w[:, here] * v[:, here])
            s[:, here] = e[:, here] - (HALF * m[:, here]) * diverge

        sweep(lo_s, hi_s, height_pass)

        def speed_pass(r, here):
            ocean, height = m[:, here], s[:, here]
            old_u, old_v = u[:, here], v[:, here]
            new_u = ocean * (KEEP * old_u + turn * old_v - (GRAVITY * HALF) * lon_diff(s, r))
            new_v = ocean * (KEEP * old_v - turn * old_u - (GRAVITY * HALF) * lat_diff(height))
            u_next[:, here] = new_u
            v_next[:, here] = new_v
            new_w = m0[:, here] + ocean * height
            w_next[:, here] = new_w
            if k < STEPS - 2:
                fe[:, here] = new_w * new_u

        sweep(lo, hi, speed_pass)

    sums = [jnp.zeros((TILES, 8, LANES), jnp.float32) for _ in range(3)]
    for k in reversed(range(STEPS)):
        u, v, w, sb = us[k], vs[k], ws[k], fe

        def height_back(r, here):
            back = le[:, here] + (GRAVITY * HALF) * (lon_diff(la, r) + lat_diff(lb[:, here]))
            sb[:, here] = back
            q[:, here] = (HALF * m[:, here]) * back

        sweep(16, 96, height_back)

        def speed_back(r, here):
            g = lon_diff(q, r)
            h = lat_diff(q[:, here])
            a, b, depth = la[:, here], lb[:, here], w[:, here]
            new_a = KEEP * a - turn * b + depth * g
            new_b = KEEP * b + turn * a + depth * h
            new_e = sb[:, here] + m[:, here] * (u[:, here] * g + v[:, here] * h)
            if k > 0:
                la[:, here] = new_a
                lb[:, here] = new_b
                le[:, here] = new_e
                return
            own = slice(r - BASE, r - BASE + 8)
            for n, new in enumerate((new_e, new_a, new_b)):
                for t in range(TILES):
                    at = slice(t * LANES, (t + 1) * LANES)
                    grad[n, own, at] = new[t] * scale[n : n + 1, at]
            half = (r - BASE) // 16 * 16
            for n, new in enumerate((new_e, new_a, new_b)):
                parts = []
                for t in range(TILES):
                    at = slice(t * LANES, (t + 1) * LANES)
                    block = stored[n, half : half + 16, at].astype(jnp.float32)
                    parts.append(new[t] * block[r - BASE - half : r - BASE - half + 8])
                sums[n] = sums[n] + jnp.stack(parts)

        if k > 0:
            sweep(16, 96, speed_back)
        else:
            sweep(BASE, BASE + COLS, speed_back)
    for n in range(3):
        partial[4 * n : 4 * n + 4] = jnp.sum(sums[n], axis=1)


def main(stored, scale, levels, mask, cot, spin, lon_a, lon_b, lat_a, lat_b):
    big = pltpu.VMEM((TILES + 1, HEIGHT, LANES), jnp.float32)
    return pl.pallas_call(
        main_kernel,
        in_specs=[pl.BlockSpec(memory_space=pltpu.VMEM)] * 10,
        out_specs=[pl.BlockSpec(memory_space=pltpu.VMEM)] * 2,
        out_shape=[
            jax.ShapeDtypeStruct((3, COLS, ROWS), jnp.float32),
            jax.ShapeDtypeStruct((3 * TILES, LANES), jnp.float32),
        ],
        scratch_shapes=[big] * 21,
        compiler_params=pltpu.CompilerParams(vmem_limit_bytes=32 * 2**20),
        name="main",
    )(stored, scale, levels, mask, cot, spin, lon_a, lon_b, lat_a, lat_b)


def spin_table():
    total = ROWS * lax.axis_size("lat")
    lane = jnp.arange((TILES + 1) * LANES, dtype=jnp.int32)
    row = jnp.where(lane < ROWS + LANES // 2, lane, lane - (TILES + 1) * LANES)
    row = (row + lax.axis_index("lat") * ROWS).astype(jnp.float32)
    spin = CORIOLIS * jnp.cos(math.pi * (row + 0.5 - total) / (2.0 * total))
    spin = jnp.broadcast_to((TIME_STEP * spin).reshape(TILES + 1, 1, LANES), (TILES + 1, 8, LANES))
    return spin


def sum_over_lon(value):
    size = lax.axis_size("lon")
    step = 1
    while step < size:
        value = value + lax.ppermute(value, "lon", [(s, s ^ step) for s in range(size)])
        step *= 2
    return value


def shards(stored, scale, levels, mask, cot):
    lons, lats = lax.axis_size("lon"), lax.axis_size("lat")
    to_a, to_b = lon_pack(stored, scale, levels, mask, cot)
    lon_a = lax.ppermute(to_a, "lon", [(s, s ^ 1) for s in range(lons)])
    lon_b = lax.ppermute(
        to_b, "lon", [(s, (s + 1) % lons if s % 2 else (s - 1) % lons) for s in range(lons)]
    )
    to_a, to_b = lat_pack(stored, scale, levels, mask, cot, lon_a, lon_b)
    lat_a = lax.ppermute(to_a, "lat", [(s, s ^ 1) for s in range(lats)])
    pairs = []
    for l in range(lons):
        for t in range(1, lats - 1, 2):
            pairs += [(l * lats + t, l * lats + t + 1), (l * lats + t + 1, l * lats + t)]
        pairs.append((l * lats + lats - 1, (lons - 1 - l) * lats + lats - 1))
    lat_b = lax.ppermute(to_b, ("lon", "lat"), pairs)
    grad, partial = main(
        stored, scale, levels, mask, cot, spin_table(), lon_a, lon_b, lat_a, lat_b
    )
    return grad, sum_over_lon(partial).reshape(3, ROWS)


def solution(mesh):
    return jax.shard_map(
        shards,
        mesh=mesh,
        in_specs=(
            P(None, "lon", "lat"),
            P(None, "lat"),
            P("lon", "lat"),
            P("lon", "lat"),
            P(None, "lon", "lat"),
        ),
        out_specs=(P(None, "lon", "lat"), P(None, "lat")),
        check_vma=False,
    )
```

time: 642 us -> 61.7 us (0.10); the launches traced: 632 us -> 61.5 us
  waiting for transfers between devices: 270 us -> 30.4 us
  blocking collectives: 187 us -> 0 us
  starting transfers between devices: 142 us -> 20.3 us
  other arithmetic: 15.1 us -> 0.07 us
  local copies, waits for them, and re-layouts: 15.9 us -> 3.14 us
  Pallas kernels: 0 us -> 6.87 us
    ppermute x90 -> x10, waiting for transfers between devices: 270 us -> 30.4 us  [the longest x6 22.9 us: sum_over_lon(): lax.ppermute(value, 'lon', [(s, s ^ step) for s in range(size)])]
    psum x1 -> x0, blocking collectives: 187 us -> none  [shards(): scale_grad = lax.psum(partial_rows, 'lon')]
    ppermute x90 -> x10, starting transfers between devices: 142 us -> 20.3 us  [the longest x1 8.72 us: shards(): lax.ppermute(to_b, 'lon', [(s, (s + 1) % lons if s % 2 else (s - 1) % lon...]
    pallas_call x0 -> x3, Pallas kernels: none -> 6.87 us  [the longest x1 2.93 us: main(): pl.pallas_call(main_kernel, in_specs=[pl.BlockSpec(memory_space=pltpu.VME...]
  transfers between devices with their start and end apart: 90 -> 10, of which waited for: 57 -> 8; matrix products, arithmetic and copies ran while one was open for 1% -> 0% of each run, Pallas kernels for 0% -> 0%
where the time goes in v1:
time: 61.7 us; the launch traced here: 61.5 us
  waiting for transfers between devices  30.4 us (49%)
  starting transfers between devices  20.3 us (33%)
  Pallas kernels  6.87 us (11%)
  local copies, waits for them, and re-layouts  3.14 us (5%)
  between operations  0.73 us (1%)
    ppermute x6, waiting for transfers between devices, sum_over_lon(): lax.ppermute(value, 'lon', [(s, s ^ step) for s in range(size)])  22.9 us
    ppermute x1, starting transfers between devices, shards(): lax.ppermute(to_b, 'lon', [(s, (s + 1) % lons if s % 2 else (s - 1) % lon...  8.72 us
    ppermute x6, starting transfers between devices, sum_over_lon(): lax.ppermute(value, 'lon', [(s, s ^ step) for s in range(size)])  6.83 us
    ppermute x1, waiting for transfers between devices, shards(): lax.ppermute(to_b, 'lon', [(s, (s + 1) % lons if s % 2 else (s - 1) % lon...  4.44 us
    ppermute x1, waiting for transfers between devices, shards(): lat_b = lax.ppermute(to_b, ('lon', 'lat'), pairs)  3.03 us
    pallas_call x1, Pallas kernels, main(): pl.pallas_call(main_kernel, in_specs=[pl.BlockSpec(memory_space=pltpu.VME...  2.93 us
    unnamed x18, local copies, waits for them, and re-layouts  2.53 us
    ppermute x1, starting transfers between devices, shards(): lat_b = lax.ppermute(to_b, ('lon', 'lat'), pairs)  2.46 us
  transfers between devices with their start and end apart: 10, of which 8 were waited for; matrix products, arithmetic and copies ran while one was open for 0% of the time, Pallas kernels for 0%

profile of v1, /device:TPU:8, one launch (start us, length us, event | category | flops | bytes accessed | tf_op | source)
XLA Modules:
  0.0 61.5 jit_solution(6330423042251354187)
XLA Ops:
  0.6 1.9 %lon_pack.1 = (f32[88,512]{1,0:T(8,128)}, f32[88,512]{1,0:T(8,128)}) custom-call(bf16[3,64,512]{2,1,0:T(8,128)(2,1)} %stored.1, bf16[3,64,512]{2,1,0:T(8,128)(2,1)} %stored.1, f32[3,512]{1,0:T(4,128)} %scale.3, s32[64,512]{1,0:T(8,128)} %levels.1, s32[64,512]{1,0:T(8,128)} %levels.1, s32[64,512]{1,0:T(8,128)} %mask.1, s32[64,512]{1,0:T(8,128)} %mask.1, ...), custom_call_target="tpu_custom_call" | custom-call | tf_op jit(solution)/shard_map/lon_pack/pallas_call | solution.py:64
  2.5 2.3 %collective-permute-start = (f32[88,512]{1,0:T(8,128)}, f32[88,512]{1,0:T(8,128)S(1)}, u32[]{:S(2)}, u32[]{:S(2)}) collective-permute-start(f32[88,512]{1,0:T(8,128)} %get-tuple-element.8), channel_id=1, source_target_pairs={{0,4},{4,0},{8,12},{12,8},{16,20},{20,16},{24,28},{28,24},{32,36},... | collective-permute-start | bytes 540680 | tf_op jit(solution)/shard_map/ppermute | solution.py:324
  4.8 8.7 %collective-permute-start.1 = (f32[88,512]{1,0:T(8,128)}, f32[88,512]{1,0:T(8,128)S(1)}, u32[]{:S(2)}, u32[]{:S(2)}) collective-permute-start(f32[88,512]{1,0:T(8,128)} %get-tuple-element.9), channel_id=1, source_target_pairs={{0,252},{4,8},{8,4},{12,16},{16,12},{20,24},{24,20},{28,32},{32,28... | collective-permute-start | bytes 540680 | tf_op jit(solution)/shard_map/ppermute | solution.py:325
  13.6 0.0 copy-start.4
  13.6 4.4 %collective-permute-done.1.b_s.b_n.lon_b = f32[88,512]{1,0:T(8,128)S(1)} collective-permute-done((f32[88,512]{1,0:T(8,128)}, f32[88,512]{1,0:T(8,128)S(1)}, u32[]{:S(2)}, u32[]{:S(2)}) %collective-permute-start.1) | collective-permute-done | bytes 180256 | tf_op jit(solution)/shard_map/ppermute | solution.py:325
  18.0 0.7 %copy-done.6 = f32[88,512]{1,0:T(8,128)} copy-done((f32[88,512]{1,0:T(8,128)}, f32[88,512]{1,0:T(8,128)S(1)}, u32[]{:S(2)}) %copy-start.6) | copy-done | bytes 180248
  18.7 2.0 %lat_pack.1 = (f32[88,128]{1,0:T(8,128)}, f32[88,128]{1,0:T(8,128)}) custom-call(bf16[3,64,512]{2,1,0:T(8,128)(2,1)} %stored.1, bf16[3,64,512]{2,1,0:T(8,128)(2,1)} %stored.1, f32[3,512]{1,0:T(4,128)} %scale.3, f32[3,512]{1,0:T(4,128)} %scale.3, s32[64,512]{1,0:T(8,128)} %levels.1, s32[64,512]{1,0:T(8,128)} %levels.1, s32[64,512]{1,0:T(8,128)} %mask.1, ...), custom_call_target="tpu_custom_call" | custom-call | tf_op jit(solution)/shard_map/lat_pack/pallas_call | solution.py:137
  20.7 2.5 %collective-permute-start.3 = (f32[88,128]{1,0:T(8,128)}, f32[88,128]{1,0:T(8,128)S(1)}, u32[]{:S(2)}, u32[]{:S(2)}) collective-permute-start(f32[88,128]{1,0:T(8,128)} %get-tuple-element.11), channel_id=1, source_target_pairs={{1,2},{2,1},{3,255},{5,6},{6,5},{7,251},{9,10},{10,9},{11,247},{13... | collective-permute-start | bytes 135176 | tf_op jit(solution)/shard_map/ppermute | solution.py:335
  23.2 0.1 fusion.5
  23.3 3.0 %collective-permute-done.3.lat_b = f32[88,128]{1,0:T(8,128)S(1)} collective-permute-done((f32[88,128]{1,0:T(8,128)}, f32[88,128]{1,0:T(8,128)S(1)}, u32[]{:S(2)}, u32[]{:S(2)}) %collective-permute-start.3) | collective-permute-done | bytes 45088 | tf_op jit(solution)/shard_map/ppermute | solution.py:335
  26.3 0.0 copy-start.5
  26.4 0.9 %copy-done.5 = f32[88,512]{1,0:T(8,128)S(1)} copy-done((f32[88,512]{1,0:T(8,128)S(1)}, f32[88,512]{1,0:T(8,128)}, u32[]{:S(2)}) %copy-start.5) | copy-done | bytes 180248
  27.3 0.9 %copy-done.7 = f32[88,512]{1,0:T(8,128)S(1)} copy-done((f32[88,512]{1,0:T(8,128)S(1)}, f32[88,512]{1,0:T(8,128)}, u32[]{:S(2)}) %copy-start.7) | copy-done | bytes 180248
  28.2 2.9 %main.1 = (f32[3,64,512]{2,1,0:T(8,128)}, f32[12,128]{1,0:T(8,128)S(1)}) custom-call(bf16[3,64,512]{2,1,0:T(8,128)(2,1)S(1)} %copy-done.1, f32[3,512]{1,0:T(4,128)S(1)} %copy-done.8, s32[64,512]{1,0:T(8,128)S(1)} %copy-done.2, s32[64,512]{1,0:T(8,128)S(1)} %copy-done.3, f32[3,64,512]{2,1,0:T(8,128)S(1)} %copy-done, f32[5,8,128]{2,1,0:T(8,128)S(1)} %broadcast_in_dim.2.spin, ...), custom_call_target="tpu_custom_call" | custom-call | tf_op jit(solution)/shard_map/main/pallas_call | solution.py:288
  31.1 5.2 %collective-permute-done.4 = f32[12,128]{1,0:T(8,128)S(1)} collective-permute-done((f32[12,128]{1,0:T(8,128)S(1)}, f32[12,128]{1,0:T(8,128)S(1)}, u32[]{:S(2)}, u32[]{:S(2)}) %collective-permute-start.4) | collective-permute-done | bytes 6176 | tf_op jit(solution)/shard_map/ppermute | solution.py:316
  36.3 3.6 %collective-permute-done.5 = f32[12,128]{1,0:T(8,128)S(1)} collective-permute-done((f32[12,128]{1,0:T(8,128)S(1)}, f32[12,128]{1,0:T(8,128)S(1)}, u32[]{:S(2)}, u32[]{:S(2)}) %collective-permute-start.5) | collective-permute-done | bytes 6176 | tf_op jit(solution)/shard_map/ppermute | solution.py:316
  39.9 0.1 collective-permute-start.6
  40.0 5.1 %collective-permute-done.6 = f32[12,128]{1,0:T(8,128)S(1)} collective-permute-done((f32[12,128]{1,0:T(8,128)S(1)}, f32[12,128]{1,0:T(8,128)S(1)}, u32[]{:S(2)}, u32[]{:S(2)}) %collective-permute-start.6) | collective-permute-done | bytes 6176 | tf_op jit(solution)/shard_map/ppermute | solution.py:316
  45.1 3.6 %collective-permute-done.7 = f32[12,128]{1,0:T(8,128)S(1)} collective-permute-done((f32[12,128]{1,0:T(8,128)S(1)}, f32[12,128]{1,0:T(8,128)S(1)}, u32[]{:S(2)}, u32[]{:S(2)}) %collective-permute-start.7) | collective-permute-done | bytes 6176 | tf_op jit(solution)/shard_map/ppermute | solution.py:316
  48.8 0.8 %collective-permute-start.8 = (f32[12,128]{1,0:T(8,128)S(1)}, f32[12,128]{1,0:T(8,128)S(1)}, u32[]{:S(2)}, u32[]{:S(2)}) collective-permute-start(f32[12,128]{1,0:T(8,128)S(1)} %add.56), channel_id=1, source_target_pairs={{0,64},{4,68},{8,72},{12,76},{16,80},{20,84},{24,88},{28,92},{32,9... | collective-permute-start | bytes 18440 | tf_op jit(solution)/shard_map/ppermute | solution.py:316
  49.6 3.7 %collective-permute-done.8 = f32[12,128]{1,0:T(8,128)S(1)} collective-permute-done((f32[12,128]{1,0:T(8,128)S(1)}, f32[12,128]{1,0:T(8,128)S(1)}, u32[]{:S(2)}, u32[]{:S(2)}) %collective-permute-start.8) | collective-permute-done | bytes 6176 | tf_op jit(solution)/shard_map/ppermute | solution.py:316
  53.3 6.0 %collective-permute-start.9 = (f32[12,128]{1,0:T(8,128)S(1)}, f32[12,128]{1,0:T(8,128)S(1)}, u32[]{:S(2)}, u32[]{:S(2)}) collective-permute-start(f32[12,128]{1,0:T(8,128)S(1)} %add.57), channel_id=1, source_target_pairs={{0,128},{4,132},{8,136},{12,140},{16,144},{20,148},{24,152},{28,15... | collective-permute-start | bytes 18440 | tf_op jit(solution)/shard_map/ppermute | solution.py:316
  59.3 1.6 %collective-permute-done.9 = f32[12,128]{1,0:T(8,128)S(1)} collective-permute-done((f32[12,128]{1,0:T(8,128)S(1)}, f32[12,128]{1,0:T(8,128)S(1)}, u32[]{:S(2)}, u32[]{:S(2)}) %collective-permute-start.9) | collective-permute-done | bytes 6176 | tf_op jit(solution)/shard_map/ppermute | solution.py:316
  60.9 0.6 reshape.26
  (26 shorter events, 0.1 us)
Async XLA Ops:
  2.5 11.0 %collective-permute-start = (f32[88,512]{1,0:T(8,128)}, f32[88,512]{1,0:T(8,128)S(1)}, u32[]{:S(2)}, u32[]{:S(2)}) collective-permute-start(f32[88,512]{1,0:T(8,128)} %get-tuple-element.8), channel_id=1, source_target_pairs={{0,4},{4,0},{8,12},{12,8},{16,20},{20,16},{24,28},{28,24},{32,36},... | collective-permute-start | bytes 540680 | tf_op jit(solution)/shard_map/ppermute | solution.py:324
  4.8 13.2 %collective-permute-start.1 = (f32[88,512]{1,0:T(8,128)}, f32[88,512]{1,0:T(8,128)S(1)}, u32[]{:S(2)}, u32[]{:S(2)}) collective-permute-start(f32[88,512]{1,0:T(8,128)} %get-tuple-element.9), channel_id=1, source_target_pairs={{0,252},{4,8},{8,4},{12,16},{16,12},{20,24},{24,20},{28,32},{32,28... | collective-permute-start | bytes 540680 | tf_op jit(solution)/shard_map/ppermute | solution.py:325
  13.6 12.8 %copy-start = (f32[3,64,512]{2,1,0:T(8,128)S(1)}, f32[3,64,512]{2,1,0:T(8,128)}, u32[]{:S(2)}) copy-start(f32[3,64,512]{2,1,0:T(8,128)} %cot.1) | copy-start | bytes 1179652
  13.6 12.8 %copy-start.1 = (bf16[3,64,512]{2,1,0:T(8,128)(2,1)S(1)}, bf16[3,64,512]{2,1,0:T(8,128)(2,1)}, u32[]{:S(2)}) copy-start(bf16[3,64,512]{2,1,0:T(8,128)(2,1)} %stored.1) | copy-start | bytes 589828
  13.6 12.8 %copy-start.2 = (s32[64,512]{1,0:T(8,128)S(1)}, s32[64,512]{1,0:T(8,128)}, u32[]{:S(2)}) copy-start(s32[64,512]{1,0:T(8,128)} %levels.1) | copy-start | bytes 393220
  13.6 12.8 %copy-start.3 = (s32[64,512]{1,0:T(8,128)S(1)}, s32[64,512]{1,0:T(8,128)}, u32[]{:S(2)}) copy-start(s32[64,512]{1,0:T(8,128)} %mask.1) | copy-start | bytes 393220
  13.6 4.5 %copy-start.4 = (f32[88,512]{1,0:T(8,128)}, f32[88,512]{1,0:T(8,128)S(1)}, u32[]{:S(2)}) copy-start(f32[88,512]{1,0:T(8,128)S(1)} %collective-permute-done.a_s.a_n.lon_a) | copy-start | bytes 540676
  18.0 0.7 %copy-start.6 = (f32[88,512]{1,0:T(8,128)}, f32[88,512]{1,0:T(8,128)S(1)}, u32[]{:S(2)}) copy-start(f32[88,512]{1,0:T(8,128)S(1)} %collective-permute-done.1.b_s.b_n.lon_b) | copy-start | bytes 540676
  20.7 2.5 %collective-permute-start.2 = (f32[88,128]{1,0:T(8,128)}, f32[88,128]{1,0:T(8,128)S(1)}, u32[]{:S(2)}, u32[]{:S(2)}) collective-permute-start(f32[88,128]{1,0:T(8,128)} %get-tuple-element.10), channel_id=1, source_target_pairs={{0,1},{1,0},{2,3},{3,2},{4,5},{5,4},{6,7},{7,6},{8,9},{9,8},{10,11... | collective-permute-start | bytes 135176 | tf_op jit(solution)/shard_map/ppermute | solution.py:329
  20.7 5.6 %collective-permute-start.3 = (f32[88,128]{1,0:T(8,128)}, f32[88,128]{1,0:T(8,128)S(1)}, u32[]{:S(2)}, u32[]{:S(2)}) collective-permute-start(f32[88,128]{1,0:T(8,128)} %get-tuple-element.11), channel_id=1, source_target_pairs={{1,2},{2,1},{3,255},{5,6},{6,5},{7,251},{9,10},{10,9},{11,247},{13... | collective-permute-start | bytes 135176 | tf_op jit(solution)/shard_map/ppermute | solution.py:335
  23.3 3.1 %copy-start.8 = (f32[3,512]{1,0:T(4,128)S(1)}, f32[3,512]{1,0:T(4,128)}, u32[]{:S(2)}) copy-start(f32[3,512]{1,0:T(4,128)} %scale.3) | copy-start | bytes 18436
  26.3 0.9 %copy-start.5 = (f32[88,512]{1,0:T(8,128)S(1)}, f32[88,512]{1,0:T(8,128)}, u32[]{:S(2)}) copy-start(f32[88,512]{1,0:T(8,128)} %copy-done.4) | copy-start | bytes 540676
  27.3 0.9 %copy-start.7 = (f32[88,512]{1,0:T(8,128)S(1)}, f32[88,512]{1,0:T(8,128)}, u32[]{:S(2)}) copy-start(f32[88,512]{1,0:T(8,128)} %copy-done.6) | copy-start | bytes 540676
  31.1 5.2 %collective-permute-start.4 = (f32[12,128]{1,0:T(8,128)S(1)}, f32[12,128]{1,0:T(8,128)S(1)}, u32[]{:S(2)}, u32[]{:S(2)}) collective-permute-start(f32[12,128]{1,0:T(8,128)S(1)} %get-tuple-element.13), channel_id=1, source_target_pairs={{0,4},{4,0},{8,12},{12,8},{16,20},{20,16},{24,28},{28,24},{32,36},... | collective-permute-start | bytes 18440 | tf_op jit(solution)/shard_map/ppermute | solution.py:316
  36.3 3.7 %collective-permute-start.5 = (f32[12,128]{1,0:T(8,128)S(1)}, f32[12,128]{1,0:T(8,128)S(1)}, u32[]{:S(2)}, u32[]{:S(2)}) collective-permute-start(f32[12,128]{1,0:T(8,128)S(1)} %add.53), channel_id=1, source_target_pairs={{0,8},{4,12},{8,0},{12,4},{16,24},{20,28},{24,16},{28,20},{32,40},... | collective-permute-start | bytes 18440 | tf_op jit(solution)/shard_map/ppermute | solution.py:316
  39.9 5.2 %collective-permute-start.6 = (f32[12,128]{1,0:T(8,128)S(1)}, f32[12,128]{1,0:T(8,128)S(1)}, u32[]{:S(2)}, u32[]{:S(2)}) collective-permute-start(f32[12,128]{1,0:T(8,128)S(1)} %add.54), channel_id=1, source_target_pairs={{0,16},{4,20},{8,24},{12,28},{16,0},{20,4},{24,8},{28,12},{32,48},... | collective-permute-start | bytes 18440 | tf_op jit(solution)/shard_map/ppermute | solution.py:316
  45.1 3.7 %collective-permute-start.7 = (f32[12,128]{1,0:T(8,128)S(1)}, f32[12,128]{1,0:T(8,128)S(1)}, u32[]{:S(2)}, u32[]{:S(2)}) collective-permute-start(f32[12,128]{1,0:T(8,128)S(1)} %add.55), channel_id=1, source_target_pairs={{0,32},{4,36},{8,40},{12,44},{16,48},{20,52},{24,56},{28,60},{32,0... | collective-permute-start | bytes 18440 | tf_op jit(solution)/shard_map/ppermute | solution.py:316
  48.8 4.5 %collective-permute-start.8 = (f32[12,128]{1,0:T(8,128)S(1)}, f32[12,128]{1,0:T(8,128)S(1)}, u32[]{:S(2)}, u32[]{:S(2)}) collective-permute-start(f32[12,128]{1,0:T(8,128)S(1)} %add.56), channel_id=1, source_target_pairs={{0,64},{4,68},{8,72},{12,76},{16,80},{20,84},{24,88},{28,92},{32,9... | collective-permute-start | bytes 18440 | tf_op jit(solution)/shard_map/ppermute | solution.py:316
  53.3 7.6 %collective-permute-start.9 = (f32[12,128]{1,0:T(8,128)S(1)}, f32[12,128]{1,0:T(8,128)S(1)}, u32[]{:S(2)}, u32[]{:S(2)}) collective-permute-start(f32[12,128]{1,0:T(8,128)S(1)} %add.57), channel_id=1, source_target_pairs={{0,128},{4,132},{8,136},{12,140},{16,144},{20,148},{24,152},{28,15... | collective-permute-start | bytes 18440 | tf_op jit(solution)/shard_map/ppermute | solution.py:316

commit v2 on v1

v2 whole, which is shorter than its diff:
```python
import math

import jax
import jax.numpy as jnp
from jax import lax
from jax.experimental import pallas as pl
from jax.experimental.pallas import tpu as pltpu
from jax.sharding import PartitionSpec as P

STEPS = 4
GRAVITY = 1.0
TIME_STEP = 0.5
LEVEL_DEPTH = 0.08
KEEP = 1.0 - 0.02
CORIOLIS = 0.1
HALF = 0.5 * TIME_STEP

COLS = 64
ROWS = 512
LANES = 128
TILES = ROWS // LANES
WIDE = 11
BASE = 24
HEIGHT = 112
SIDE = 76
BULK = SIDE * TILES

LON_WIDTHS = (11, 11, 11, 11, 10, 7, 8, 7)
LAT_WIDTHS = (11, 11, 11, 10, 11, 7, 7, 8)
LON_PLACES = tuple(sum(LON_WIDTHS[:f]) for f in range(8))
LAT_PLACES = tuple(sum(LAT_WIDTHS[:f]) for f in range(8))
SIGNS = (1.0, 1.0, 1.0, -1.0, -1.0, 1.0, -1.0, -1.0)
VMEM = pl.BlockSpec(memory_space=pltpu.VMEM)
SMALL = pltpu.CompilerParams(vmem_limit_bytes=4 * 2**20)


def lanes_of(shape):
    return lax.broadcasted_iota(jnp.int32, shape, len(shape) - 1)


def own_fields(stored, scale, levels, mask, cot):
    ocean = mask.astype(jnp.float32)
    floor = ocean * (LEVEL_DEPTH * levels.astype(jnp.float32))
    state = [stored[k].astype(jnp.float32) * scale[k : k + 1] for k in range(3)]
    return [ocean, floor] + state + [cot[0], ocean * cot[1], ocean * cot[2]]


def lat_pack_kernel(
    stored, scale, levels, mask, cot, out_a, out_b, st, sc, lev, ocean, adj, sems
):
    arrays = ((stored, st), (scale, sc), (levels, lev), (mask, ocean), (cot, adj))
    copies = []
    for tile in (0, TILES - 1):
        for n, (src, dst) in enumerate(arrays):
            side = min(tile, 1)
            at = pl.ds(tile * LANES, LANES)
            copies.append(
                pltpu.make_async_copy(
                    src.at[(slice(None),) * (len(src.shape) - 1) + (at,)],
                    dst.at[side],
                    sems.at[side, n],
                )
            )
    for copy in copies:
        copy.start()
    lat = lax.axis_index("lat")
    upper = lax.rem(lat, 2) == 1
    top = lat == lax.axis_size("lat") - 1
    for copy in copies:
        copy.wait()
    packs = []
    for side, to_south in ((0, True), (1, False)):
        fields = own_fields(st[side], sc[side], lev[side], ocean[side], adj[side])
        total = jnp.zeros((COLS, LANES), jnp.float32)
        lane = lanes_of(total.shape)
        for f in range(8):
            width, place = LAT_WIDTHS[f], LAT_PLACES[f]
            shift = place if to_south else (place + width) % LANES
            moved = fields[f] if shift == 0 else pltpu.roll(fields[f], shift, 1)
            total = jnp.where((lane >= place) & (lane < place + width), moved, total)
        packs.append(total)
    south, north = packs
    out_a[...] = jnp.where(upper, south, north)
    out_b[...] = jnp.where(upper, north, south)

    @pl.when(top)
    def _():
        i = lax.broadcasted_iota(jnp.int32, (COLS, COLS), 0)
        j = lax.broadcasted_iota(jnp.int32, (COLS, COLS), 1)
        flip_cols = jnp.where(i + j == COLS - 1, 1.0, 0.0)
        i = lax.broadcasted_iota(jnp.int32, (LANES, LANES), 0)
        j = lax.broadcasted_iota(jnp.int32, (LANES, LANES), 1)
        flip_rows = jnp.zeros((LANES, LANES), jnp.float32)
        for f in range(8):
            first, last = LAT_PLACES[f], LAT_PLACES[f] + LAT_WIDTHS[f] - 1
            here = (i >= first) & (i <= last) & (i + j == first + last)
            flip_rows = jnp.where(here, SIGNS[f], flip_rows)
        exact = dict(precision=lax.Precision.HIGHEST, preferred_element_type=jnp.float32)
        out_b[...] = jnp.dot(flip_cols, jnp.dot(out_b[...], flip_rows, **exact), **exact)


def lat_pack(*own):
    out = jax.ShapeDtypeStruct((COLS, LANES), jnp.float32)
    return pl.pallas_call(
        lat_pack_kernel,
        in_specs=[pl.BlockSpec(memory_space=pltpu.HBM)] * 5,
        out_specs=[VMEM] * 2,
        out_shape=[out, out],
        scratch_shapes=[
            pltpu.VMEM((2, 3, COLS, LANES), jnp.bfloat16),
            pltpu.VMEM((2, 3, LANES), jnp.float32),
            pltpu.VMEM((2, COLS, LANES), jnp.int32),
            pltpu.VMEM((2, COLS, LANES), jnp.int32),
            pltpu.VMEM((2, 3, COLS, LANES), jnp.float32),
            pltpu.SemaphoreType.DMA((2, 5)),
        ],
        compiler_params=pltpu.CompilerParams(vmem_limit_bytes=55100 * 2**10),
        name="lat_pack",
    )(*own)


def lon_pack_kernel(*refs):
    srcs, (a_ref, b_ref), dsts, sems = refs[:5], refs[6:8], refs[8:13], refs[13]
    copies = [pltpu.make_async_copy(srcs[n], dsts[n], sems.at[n]) for n in range(5)]
    for copy in copies:
        copy.start()
    odd = lax.rem(lax.axis_index("lon"), 2) == 1
    for copy in copies:
        copy.wait()
    stored, scale, levels, mask, cot = dsts
    for t in range(TILES):
        at = slice(t * LANES, (t + 1) * LANES)
        low, high = (
            own_fields(
                stored[:, cut, at], scale[:, at], levels[cut, at], mask[cut, at], cot[:, cut, at]
            )
            for cut in (slice(0, 16), slice(COLS - 16, COLS))
        )
        for f in range(8):
            width, place = LON_WIDTHS[f], t * SIDE + LON_PLACES[f]
            lower, upper = low[f][:width], high[f][16 - width :]
            a_ref[place : place + width] = jnp.where(odd, lower, upper)
            b_ref[place : place + width] = jnp.where(odd, upper, lower)


def lon_pack(own, after):
    out = jax.ShapeDtypeStruct((BULK, LANES), jnp.float32)
    outs = pl.pallas_call(
        lon_pack_kernel,
        in_specs=[pl.BlockSpec(memory_space=pltpu.HBM)] * 6,
        out_specs=[VMEM] * 7,
        out_shape=[out, out] + [jax.ShapeDtypeStruct(x.shape, x.dtype) for x in own],
        scratch_shapes=[pltpu.SemaphoreType.DMA((5,))],
        compiler_params=SMALL,
        name="lon_pack",
        cost_estimate=pl.CostEstimate(flops=10**6, bytes_accessed=10**6, transcendentals=0),
    )(*own, after)
    return outs[:2], outs[2:]


def corner_pack_kernel(lat_a, lat_b, a_in, b_in, a_ref, b_ref):
    odd = lax.rem(lax.axis_index("lon"), 2) == 1
    for n, margin in enumerate((lat_a, lat_b)):
        lower, upper = margin[:WIDE], margin[COLS - WIDE :]
        rows = slice(BULK + n * WIDE, BULK + (n + 1) * WIDE)
        a_ref[rows] = jnp.where(odd, lower, upper)
        b_ref[rows] = jnp.where(odd, upper, lower)
    for src, ref in ((a_in, a_ref), (b_in, b_ref)):
        ref[:BULK] = src[...]
        ref[BULK + 2 * WIDE :] = jnp.zeros((24 - 2 * WIDE, LANES), jnp.float32)


def corner_pack(lat_a, lat_b, to_a, to_b):
    out = jax.ShapeDtypeStruct((BULK + 24, LANES), jnp.float32)
    return pl.pallas_call(
        corner_pack_kernel,
        in_specs=[VMEM] * 4,
        out_specs=[VMEM] * 2,
        out_shape=[out, out],
        compiler_params=SMALL,
        name="corner_pack",
    )(lat_a, lat_b, to_a, to_b)


def main_kernel(
    stored, scale, levels, mask, cot, spin, lat_a, lat_b, lon_a, lon_b,
    lam, partial,
    m, m0, u0, u1, u2, u3, v0, v1, v2, v3, w0, w1, w2, w3, ea, eb, fe, q, la, lb, le,
    north, south,
):
    odd = lax.rem(lax.axis_index("lon"), 2) == 1
    upper = lax.rem(lax.axis_index("lat"), 2) == 1
    us, vs, ws = (u0, u1, u2, u3), (v0, v1, v2, v3), (w0, w1, w2, w3)
    fields = (m, m0, ea, u0, v0, le, la, lb)
    every = TILES + 1
    end = BASE + COLS

    for f in range(8):
        for row in (slice(0, 16), slice(96, HEIGHT)):
            fields[f][:, row] = jnp.zeros((every, 16, LANES), jnp.float32)
        for row in (slice(16, 24), slice(88, 96)):
            fields[f][:, row] = jnp.zeros((every, 8, LANES), jnp.float32)
    for t in range(TILES):
        at = slice(t * LANES, (t + 1) * LANES)
        own = own_fields(
            stored[:, :, at], scale[:, at], levels[:, at], mask[:, at], cot[:, :, at]
        )
        for f in range(8):
            fields[f][t, BASE:end] = own[f]
            width, place = LON_WIDTHS[f], t * SIDE + LON_PLACES[f]
            from_a, from_b = lon_a[place : place + width], lon_b[place : place + width]
            fields[f][t, BASE - width : BASE] = jnp.where(odd, from_a, from_b)
            fields[f][t, end : end + width] = jnp.where(odd, from_b, from_a)
    for n, (ref, own) in enumerate(((lat_a, lat_b), (lat_b, lat_a))):
        dst = (north, south)[n]
        dst[BASE:end] = jnp.where(upper, own[...], ref[...])
        first, second = (slice(BULK + k * WIDE, BULK + (k + 1) * WIDE) for k in (n, 1 - n))
        from_a = jnp.where(upper, lon_a[second], lon_a[first])
        from_b = jnp.where(upper, lon_b[second], lon_b[first])
        dst[BASE - WIDE : BASE] = jnp.where(odd, from_a, from_b)
        dst[end : end + WIDE] = jnp.where(odd, from_b, from_a)
    lane = lanes_of((COLS + 2 * WIDE, LANES))
    packs = [ref[BASE - WIDE : end + WIDE] for ref in (north, south)]
    for f in range(8):
        width, place = LAT_WIDTHS[f], LAT_PLACES[f]
        up = pltpu.roll(packs[0], (LANES - place) % LANES, 1) if place else packs[0]
        down = pltpu.roll(packs[1], LANES - width - place, 1)
        edge = jnp.where(lane < width, up, jnp.where(lane >= LANES - width, down, 0.0))
        fields[f][TILES, BASE - WIDE : end + WIDE] = edge

    first = lanes_of((every, 8, LANES)) == 0
    final = lanes_of((every, 8, LANES)) == LANES - 1

    def lat_diff(x):
        ahead = pltpu.roll(x, LANES - 1, 2)
        behind = pltpu.roll(x, 1, 2)
        ahead = jnp.where(final, jnp.concatenate([ahead[1:], ahead[:1]], axis=0), ahead)
        behind = jnp.where(first, jnp.concatenate([behind[-1:], behind[:-1]], axis=0), behind)
        return ahead - behind

    def lon_diff(ref, r):
        return ref[:, pl.ds(r + 1, 8)] - ref[:, pl.ds(r - 1, 8)]

    def sweep(start, stop, body):
        for r in range(start, stop, 8):
            body(r, pl.ds(r, 8))

    turn = spin[...]

    def start_step(r, here):
        w = m0[:, here] + m[:, here] * ea[:, here]
        w0[:, here] = w
        fe[:, here] = w * u0[:, here]

    sweep(8, 104, start_step)

    for k in range(STEPS - 1):
        e, s = (ea, eb) if k % 2 == 0 else (eb, ea)
        u, v, w, u_next, v_next, w_next = us[k], vs[k], ws[k], us[k + 1], vs[k + 1], ws[k + 1]
        lo, hi = ((8, 104), (8, 104), (16, 96))[k]
        lo_s, hi_s = ((8, 104), (8, 104), (16, 96))[k]
        if k == 1:
            lo, hi = 16, 96

        def height_pass(r, here):
            diverge = lon_diff(fe, r) + lat_diff(w[:, here] * v[:, here])
            s[:, here] = e[:, here] - (HALF * m[:, here]) * diverge

        sweep(lo_s, hi_s, height_pass)

        def speed_pass(r, here):
            ocean, height = m[:, here], s[:, here]
            old_u, old_v = u[:, here], v[:, here]
            new_u = ocean * (KEEP * old_u + turn * old_v - (GRAVITY * HALF) * lon_diff(s, r))
            new_v = ocean * (KEEP * old_v - turn * old_u - (GRAVITY * HALF) * lat_diff(height))
            u_next[:, here] = new_u
            v_next[:, here] = new_v
            new_w = m0[:, here] + ocean * height
            w_next[:, here] = new_w
            if k < STEPS - 2:
                fe[:, here] = new_w * new_u

        sweep(lo, hi, speed_pass)

    sums = [jnp.zeros((TILES, 8, LANES), jnp.float32) for _ in range(3)]
    for k in reversed(range(STEPS)):
        u, v, w, sb = us[k], vs[k], ws[k], fe

        def height_back(r, here):
            back = le[:, here] + (GRAVITY * HALF) * (lon_diff(la, r) + lat_diff(lb[:, here]))
            sb[:, here] = back
            q[:, here] = (HALF * m[:, here]) * back

        sweep(16, 96, height_back)

        def speed_back(r, here):
            g = lon_diff(q, r)
            h = lat_diff(q[:, here])
            a, b, depth = la[:, here], lb[:, here], w[:, here]
            new_a = KEEP * a - turn * b + depth * g
            new_b = KEEP * b + turn * a + depth * h
            new_e = sb[:, here] + m[:, here] * (u[:, here] * g + v[:, here] * h)
            if k > 0:
                la[:, here] = new_a
                lb[:, here] = new_b
                le[:, here] = new_e
                return
            own = slice(r - BASE, r - BASE + 8)
            for n, new in enumerate((new_e, new_a, new_b)):
                for t in range(TILES):
                    at = slice(t * LANES, (t + 1) * LANES)
                    lam[n, own, at] = new[t]
            half = (r - BASE) // 16 * 16
            for n, new in enumerate((new_e, new_a, new_b)):
                parts = []
                for t in range(TILES):
                    at = slice(t * LANES, (t + 1) * LANES)
                    block = stored[n, half : half + 16, at].astype(jnp.float32)
                    parts.append(new[t] * block[r - BASE - half : r - BASE - half + 8])
                sums[n] = sums[n] + jnp.stack(parts)

        if k > 0:
            sweep(16, 96, speed_back)
        else:
            sweep(BASE, BASE + COLS, speed_back)
    for n in range(3):
        total = jnp.sum(sums[n], axis=1)
        for t in range(TILES):
            partial[n : n + 1, t * LANES : (t + 1) * LANES] = total[t : t + 1]


def main(*operands):
    big = pltpu.VMEM((TILES + 1, HEIGHT, LANES), jnp.float32)
    return pl.pallas_call(
        main_kernel,
        in_specs=[VMEM] * 10,
        out_specs=[VMEM] * 2,
        out_shape=[
            jax.ShapeDtypeStruct((3, COLS, ROWS), jnp.float32),
            jax.ShapeDtypeStruct((3, ROWS), jnp.float32),
        ],
        scratch_shapes=[big] * 21 + [pltpu.VMEM((HEIGHT, LANES), jnp.float32)] * 2,
        compiler_params=pltpu.CompilerParams(vmem_limit_bytes=12 * 2**20),
        name="main",
    )(*operands)


def spin_table():
    total = ROWS * lax.axis_size("lat")
    lane = jnp.arange((TILES + 1) * LANES, dtype=jnp.int32)
    row = jnp.where(lane < ROWS + LANES // 2, lane, lane - (TILES + 1) * LANES)
    row = (row + lax.axis_index("lat") * ROWS).astype(jnp.float32)
    spin = CORIOLIS * jnp.cos(math.pi * (row + 0.5 - total) / (2.0 * total))
    spin = jnp.broadcast_to((TIME_STEP * spin).reshape(TILES + 1, 1, LANES), (TILES + 1, 8, LANES))
    return spin


def sum_over_lon(value):
    size = lax.axis_size("lon")
    columns = [[z * 8 + r for z in range(size // 8)] for r in range(8)]
    many = jnp.broadcast_to(value[None], (size // 8,) + value.shape)
    many = lax.all_to_all(many, "lon", 0, 0, axis_index_groups=columns)
    value = jnp.sum(many, axis=0)
    for steps in ((1,), (2, 4, 6)):
        value = value + sum(
            lax.ppermute(value, "lon", [(s, s ^ step) for s in range(size)]) for step in steps
        )
    return value


def shards(stored, scale, levels, mask, cot):
    lons, lats = lax.axis_size("lon"), lax.axis_size("lat")
    own = (stored, scale, levels, mask, cot)
    to_a, to_b = lat_pack(*own)
    lat_a = lax.ppermute(to_a, "lat", [(s, s ^ 1) for s in range(lats)])
    pairs = []
    for l in range(lons):
        for t in range(1, lats - 1, 2):
            pairs += [(l * lats + t, l * lats + t + 1), (l * lats + t + 1, l * lats + t)]
        pairs.append((l * lats + lats - 1, (lons - 1 - l) * lats + lats - 1))
    lat_b = lax.ppermute(to_b, ("lon", "lat"), pairs)
    bulk, near = lon_pack(own, to_b)
    to_a, to_b = corner_pack(lat_a, lat_b, *bulk)
    lon_a = lax.ppermute(to_a, "lon", [(s, s ^ 1) for s in range(lons)])
    lon_b = lax.ppermute(
        to_b, "lon", [(s, (s + 1) % lons if s % 2 else (s - 1) % lons) for s in range(lons)]
    )
    lam, partial = main(*near, spin_table(), lat_a, lat_b, lon_a, lon_b)
    return lam * near[1][:, None, :], sum_over_lon(partial)


def solution(mesh):
    return jax.shard_map(
        shards,
        mesh=mesh,
        in_specs=(
            P(None, "lon", "lat"),
            P(None, "lat"),
            P("lon", "lat"),
            P("lon", "lat"),
            P(None, "lon", "lat"),
        ),
        out_specs=(P(None, "lon", "lat"), P(None, "lat")),
        check_vma=False,
    )
```

time: 61.7 us -> 53.9 us (0.87)
  the two profiles are of different devices: /device:TPU:8 before, /device:TPU:25 now
where the time goes in v2:
time: 53.9 us; the launch traced here: 53.7 us
  starting transfers between devices  21.5 us (40%)
  blocking collectives  14.4 us (27%)
  waiting for transfers between devices  9.94 us (18%)
  Pallas kernels  4.83 us (9%)
  other arithmetic  1.48 us (3%)
  local copies, waits for them, and re-layouts  0.78 us (1%)
  between operations  0.76 us (1%)
    all_to_all x1, blocking collectives, sum_over_lon(): many = lax.all_to_all(many, 'lon', 0, 0, axis_index_groups=columns)  14.4 us
    ppermute x1, starting transfers between devices, shards(): lat_b = lax.ppermute(to_b, ('lon', 'lat'), pairs)  10.3 us
    ppermute x4, starting transfers between devices, sum_over_lon(): lax.ppermute(value, 'lon', [(s, s ^ step) for s in range(size)])  8.14 us
    ppermute x4, waiting for transfers between devices, sum_over_lon(): lax.ppermute(value, 'lon', [(s, s ^ step) for s in range(size)])  3.58 us
    ppermute x1, waiting for transfers between devices, shards(): lon_a = lax.ppermute(to_a, 'lon', [(s, s ^ 1) for s in range(lons)])  3.43 us
    ppermute x1, waiting for transfers between devices, shards(): lax.ppermute(to_b, 'lon', [(s, (s + 1) % lons if s % 2 else (s - 1) % lon...  2.51 us
    pallas_call x1, Pallas kernels, main(): pl.pallas_call(main_kernel, in_specs=[VMEM] * 10, out_specs=[VMEM] * 2, o...  2.14 us
    ppermute x1, starting transfers between devices, shards(): lon_a = lax.ppermute(to_a, 'lon', [(s, s ^ 1) for s in range(lons)])  2 us
  transfers between devices with their start and end apart: 8, of which 5 were waited for; matrix products, arithmetic and copies ran while one was open for 2% of the time, Pallas kernels for 2%

profile of v2, /device:TPU:25, one launch (start us, length us, event | category | flops | bytes accessed | tf_op | source)
XLA Modules:
  0.0 53.7 jit_solution(3727987930334071588)
XLA Ops:
  0.7 0.7 %copy-done.4 = f32[3,512]{1,0:T(4,128)S(1)} copy-done((f32[3,512]{1,0:T(4,128)S(1)}, f32[3,512]{1,0:T(4,128)}, u32[]{:S(2)}) %copy-start.4) | copy-done | bytes 6168
  1.4 1.8 %lat_pack.1 = (f32[64,128]{1,0:T(8,128)S(1)}, f32[64,128]{1,0:T(8,128)S(1)}) custom-call(bf16[3,64,512]{2,1,0:T(8,128)(2,1)} %refs_0_.1, f32[3,512]{1,0:T(4,128)S(1)} %copy-done.4, s32[64,512]{1,0:T(8,128)} %refs_2_.1, s32[64,512]{1,0:T(8,128)} %refs_3_.1, f32[3,64,512]{2,1,0:T(8,128)} %refs_4_.1), custom_call_target="tpu_custom_call" | custom-call | tf_op jit(solution)/shard_map/lat_pack/pallas_call | solution.py:104
  3.2 0.4 collective-permute-start
  3.6 10.3 %collective-permute-start.1 = (f32[64,128]{1,0:T(8,128)S(1)}, f32[64,128]{1,0:T(8,128)S(1)}, u32[]{:S(2)}, u32[]{:S(2)}) collective-permute-start(f32[64,128]{1,0:T(8,128)S(1)} %get-tuple-element.15.refs_5_), channel_id=1, source_target_pairs={{1,2},{2,1},{3,255},{5,6},{6,5},{7,251},{9,10},{10,9},{11,247},{13... | collective-permute-start | bytes 98312 | tf_op jit(solution)/shard_map/ppermute | solution.py:381
  14.0 0.9 %lon_pack.1 = (f32[304,128]{1,0:T(8,128)S(1)}, f32[304,128]{1,0:T(8,128)S(1)}, bf16[3,64,512]{2,1,0:T(8,128)(2,1)S(1)}, f32[3,512]{1,0:T(4,128)S(1)}, s32[64,512...) custom-call(bf16[3,64,512]{2,1,0:T(8,128)(2,1)S(1)} %copy-done.1, f32[3,512]{1,0:T(4,128)S(1)} %copy-done.4, ...), custom_call_target="tpu_custom_call" | custom-call | flops 1000000 | bytes 1000000 | tf_op jit(solution)/shard_map/lon_pack/pallas_call | solution.py:148
  14.9 0.0 collective-permute-done.lat_a
  14.9 0.4 collective-permute-done.1.lat_b
  15.3 2.0 %collective-permute-start.2 = (f32[328,128]{1,0:T(8,128)S(1)}, f32[328,128]{1,0:T(8,128)S(1)}, u32[]{:S(2)}, u32[]{:S(2)}) collective-permute-start(f32[328,128]{1,0:T(8,128)S(1)} %get-tuple-element.24), channel_id=1, source_target_pairs={{0,4},{4,0},{8,12},{12,8},{16,20},{20,16},{24,28},{28,24},{32,36},... | collective-permute-start | bytes 503816 | tf_op jit(solution)/shard_map/ppermute | solution.py:384
  17.3 0.6 %collective-permute-start.3 = (f32[328,128]{1,0:T(8,128)S(1)}, f32[328,128]{1,0:T(8,128)S(1)}, u32[]{:S(2)}, u32[]{:S(2)}) collective-permute-start(f32[328,128]{1,0:T(8,128)S(1)} %get-tuple-element.25), channel_id=1, source_target_pairs={{0,252},{4,8},{8,4},{12,16},{16,12},{20,24},{24,20},{28,32},{32,28... | collective-permute-start | bytes 503816 | tf_op jit(solution)/shard_map/ppermute | solution.py:385
  18.0 0.1 fusion.5
  18.0 3.4 %collective-permute-done.2.lon_a = f32[328,128]{1,0:T(8,128)S(1)} collective-permute-done((f32[328,128]{1,0:T(8,128)S(1)}, f32[328,128]{1,0:T(8,128)S(1)}, u32[]{:S(2)}, u32[]{:S(2)}) %collective-permute-start.2) | collective-permute-done | bytes 167968 | tf_op jit(solution)/shard_map/ppermute | solution.py:384
  21.5 2.5 %collective-permute-done.3.lon_b = f32[328,128]{1,0:T(8,128)S(1)} collective-permute-done((f32[328,128]{1,0:T(8,128)S(1)}, f32[328,128]{1,0:T(8,128)S(1)}, u32[]{:S(2)}, u32[]{:S(2)}) %collective-permute-start.3) | collective-permute-done | bytes 167968 | tf_op jit(solution)/shard_map/ppermute | solution.py:385
  24.0 2.1 %main.1 = (f32[3,64,512]{2,1,0:T(8,128)S(1)}, f32[3,512]{1,0:T(4,128)S(1)}) custom-call(bf16[3,64,512]{2,1,0:T(8,128)(2,1)S(1)} %get-tuple-element.16.stored, f32[3,512]{1,0:T(4,128)S(1)} %get-tuple-element.17.scale, s32[64,512]{1,0:T(8,128)S(1)} %get-tuple-element.18.levels, s32[64,512]{1,0:T(8,128)S(1)} %get-tuple-element.19.mask, ...), custom_call_target="tpu_custom_call" | custom-call | tf_op jit(solution)/shard_map/main/pallas_call | solution.py:334
  26.1 14.4 %all_to_all.5 = f32[8,3,512]{2,1,0:T(4,128)S(1)} all-to-all(f32[8,3,512]{2,1,0:T(4,128)S(1)} %broadcast_in_dim.5), channel_id=1, replica_groups={{0,32,64,96,128,160,192,224},{4,36,68,100,132,164,196,228},{8,40,72,104..., dimensions={0} | all-to-all | bytes 98304 | tf_op jit(solution)/shard_map/all_to_all | solution.py:362
  40.6 4.3 %collective-permute-start.4 = (f32[3,512]{1,0:T(4,128)S(1)}, f32[3,512]{1,0:T(4,128)S(1)}, u32[]{:S(2)}, u32[]{:S(2)}) collective-permute-start(f32[3,512]{1,0:T(4,128)S(1)} %reduce_sum.9), channel_id=1, source_target_pairs={{0,4},{4,0},{8,12},{12,8},{16,20},{20,16},{24,28},{28,24},{32,36},... | collective-permute-start | bytes 18440 | tf_op jit(solution)/shard_map/ppermute | solution.py:366
  44.8 1.0 %collective-permute-done.4 = f32[3,512]{1,0:T(4,128)S(1)} collective-permute-done((f32[3,512]{1,0:T(4,128)S(1)}, f32[3,512]{1,0:T(4,128)S(1)}, u32[]{:S(2)}, u32[]{:S(2)}) %collective-permute-start.4) | collective-permute-done | bytes 6176 | tf_op jit(solution)/shard_map/ppermute | solution.py:366
  45.9 3.2 %collective-permute-start.7 = (f32[3,512]{1,0:T(4,128)S(1)}, f32[3,512]{1,0:T(4,128)S(1)}, u32[]{:S(2)}, u32[]{:S(2)}) collective-permute-start(f32[3,512]{1,0:T(4,128)S(1)} %add.47), channel_id=1, source_target_pairs={{0,24},{4,28},{8,16},{12,20},{16,8},{20,12},{24,0},{28,4},{32,56},... | collective-permute-start | bytes 18440 | tf_op jit(solution)/shard_map/ppermute | solution.py:366
  49.1 0.0 collective-permute-start.6
  49.1 0.7 %collective-permute-start.5 = (f32[3,512]{1,0:T(4,128)S(1)}, f32[3,512]{1,0:T(4,128)S(1)}, u32[]{:S(2)}, u32[]{:S(2)}) collective-permute-start(f32[3,512]{1,0:T(4,128)S(1)} %add.47), channel_id=1, source_target_pairs={{0,8},{4,12},{8,0},{12,4},{16,24},{20,28},{24,16},{28,20},{32,40},... | collective-permute-start | bytes 18440 | tf_op jit(solution)/shard_map/ppermute | solution.py:366
  49.7 0.8 %broadcast_multiply_fusion = f32[3,64,512]{2,1,0:T(8,128)} fusion(f32[3,64,512]{2,1,0:T(8,128)S(1)} %get-tuple-element.26, f32[3,512]{1,0:T(4,128)S(1)} %get-tuple-element.17.scale), kind=kLoop, calls=%fused_computation | loop fusion | flops 98304 | bytes 792576 | tf_op jit(solution)/shard_map/mul | solution.py:389
  50.5 0.0 collective-permute-done.7
  50.5 2.5 %collective-permute-done.6 = f32[3,512]{1,0:T(4,128)S(1)} collective-permute-done((f32[3,512]{1,0:T(4,128)S(1)}, f32[3,512]{1,0:T(4,128)S(1)}, u32[]{:S(2)}, u32[]{:S(2)}) %collective-permute-start.6) | collective-permute-done | bytes 6176 | tf_op jit(solution)/shard_map/ppermute | solution.py:366
  53.1 0.0 collective-permute-done.5
  53.1 0.6 %add_add_fusion = f32[3,512]{1,0:T(4,128)} fusion(f32[3,512]{1,0:T(4,128)S(1)} %add.47, f32[3,512]{1,0:T(4,128)S(1)} %collective-permute-done.7, f32[3,512]{1,0:T(4,128)S(1)} %collective-permute-done.5, f32[3,512]{1,0:T(4,128)S(1)} %collective-permute-done.6), kind=kLoop, calls=%fused_computation.2 | loop fusion | flops 4608 | bytes 30720 | tf_op jit(solution)/shard_map/add | solution.py:365
  (14 shorter events, 0.1 us)
Async XLA Ops:
  0.6 13.3 %copy-start = (f32[3,64,512]{2,1,0:T(8,128)S(1)}, f32[3,64,512]{2,1,0:T(8,128)}, u32[]{:S(2)}) copy-start(f32[3,64,512]{2,1,0:T(8,128)} %refs_4_.1) | copy-start | bytes 1179652
  0.6 13.3 %copy-start.3 = (s32[64,512]{1,0:T(8,128)S(1)}, s32[64,512]{1,0:T(8,128)}, u32[]{:S(2)}) copy-start(s32[64,512]{1,0:T(8,128)} %refs_3_.1) | copy-start | bytes 393220
  0.7 13.3 %copy-start.2 = (s32[64,512]{1,0:T(8,128)S(1)}, s32[64,512]{1,0:T(8,128)}, u32[]{:S(2)}) copy-start(s32[64,512]{1,0:T(8,128)} %refs_2_.1) | copy-start | bytes 393220
  0.7 0.8 %copy-start.4 = (f32[3,512]{1,0:T(4,128)S(1)}, f32[3,512]{1,0:T(4,128)}, u32[]{:S(2)}) copy-start(f32[3,512]{1,0:T(4,128)} %refs_1_.1) | copy-start | bytes 18436
  1.4 12.5 %copy-start.1 = (bf16[3,64,512]{2,1,0:T(8,128)(2,1)S(1)}, bf16[3,64,512]{2,1,0:T(8,128)(2,1)}, u32[]{:S(2)}) copy-start(bf16[3,64,512]{2,1,0:T(8,128)(2,1)} %refs_0_.1) | copy-start | bytes 589828
  3.2 11.7 %collective-permute-start = (f32[64,128]{1,0:T(8,128)S(1)}, f32[64,128]{1,0:T(8,128)S(1)}, u32[]{:S(2)}, u32[]{:S(2)}) collective-permute-start(f32[64,128]{1,0:T(8,128)S(1)} %get-tuple-element.21), channel_id=1, source_target_pairs={{0,1},{1,0},{2,3},{3,2},{4,5},{5,4},{6,7},{7,6},{8,9},{9,8},{10,11... | collective-permute-start | bytes 98312 | tf_op jit(solution)/shard_map/ppermute | solution.py:375
  3.6 11.7 %collective-permute-start.1 = (f32[64,128]{1,0:T(8,128)S(1)}, f32[64,128]{1,0:T(8,128)S(1)}, u32[]{:S(2)}, u32[]{:S(2)}) collective-permute-start(f32[64,128]{1,0:T(8,128)S(1)} %get-tuple-element.15.refs_5_), channel_id=1, source_target_pairs={{1,2},{2,1},{3,255},{5,6},{6,5},{7,251},{9,10},{10,9},{11,247},{13... | collective-permute-start | bytes 98312 | tf_op jit(solution)/shard_map/ppermute | solution.py:381
  15.3 6.1 %collective-permute-start.2 = (f32[328,128]{1,0:T(8,128)S(1)}, f32[328,128]{1,0:T(8,128)S(1)}, u32[]{:S(2)}, u32[]{:S(2)}) collective-permute-start(f32[328,128]{1,0:T(8,128)S(1)} %get-tuple-element.24), channel_id=1, source_target_pairs={{0,4},{4,0},{8,12},{12,8},{16,20},{20,16},{24,28},{28,24},{32,36},... | collective-permute-start | bytes 503816 | tf_op jit(solution)/shard_map/ppermute | solution.py:384
  17.3 6.6 %collective-permute-start.3 = (f32[328,128]{1,0:T(8,128)S(1)}, f32[328,128]{1,0:T(8,128)S(1)}, u32[]{:S(2)}, u32[]{:S(2)}) collective-permute-start(f32[328,128]{1,0:T(8,128)S(1)} %get-tuple-element.25), channel_id=1, source_target_pairs={{0,252},{4,8},{8,4},{12,16},{16,12},{20,24},{24,20},{28,32},{32,28... | collective-permute-start | bytes 503816 | tf_op jit(solution)/shard_map/ppermute | solution.py:385
  40.6 5.3 %collective-permute-start.4 = (f32[3,512]{1,0:T(4,128)S(1)}, f32[3,512]{1,0:T(4,128)S(1)}, u32[]{:S(2)}, u32[]{:S(2)}) collective-permute-start(f32[3,512]{1,0:T(4,128)S(1)} %reduce_sum.9), channel_id=1, source_target_pairs={{0,4},{4,0},{8,12},{12,8},{16,20},{20,16},{24,28},{28,24},{32,36},... | collective-permute-start | bytes 18440 | tf_op jit(solution)/shard_map/ppermute | solution.py:366
  45.9 4.7 %collective-permute-start.7 = (f32[3,512]{1,0:T(4,128)S(1)}, f32[3,512]{1,0:T(4,128)S(1)}, u32[]{:S(2)}, u32[]{:S(2)}) collective-permute-start(f32[3,512]{1,0:T(4,128)S(1)} %add.47), channel_id=1, source_target_pairs={{0,24},{4,28},{8,16},{12,20},{16,8},{20,12},{24,0},{28,4},{32,56},... | collective-permute-start | bytes 18440 | tf_op jit(solution)/shard_map/ppermute | solution.py:366
  49.1 4.0 %collective-permute-start.6 = (f32[3,512]{1,0:T(4,128)S(1)}, f32[3,512]{1,0:T(4,128)S(1)}, u32[]{:S(2)}, u32[]{:S(2)}) collective-permute-start(f32[3,512]{1,0:T(4,128)S(1)} %add.47), channel_id=1, source_target_pairs={{0,16},{4,20},{8,24},{12,28},{16,0},{20,4},{24,8},{28,12},{32,48},... | collective-permute-start | bytes 18440 | tf_op jit(solution)/shard_map/ppermute | solution.py:366
  49.1 4.0 %collective-permute-start.5 = (f32[3,512]{1,0:T(4,128)S(1)}, f32[3,512]{1,0:T(4,128)S(1)}, u32[]{:S(2)}, u32[]{:S(2)}) collective-permute-start(f32[3,512]{1,0:T(4,128)S(1)} %add.47), channel_id=1, source_target_pairs={{0,8},{4,12},{8,0},{12,4},{16,24},{20,28},{24,16},{28,20},{32,40},... | collective-permute-start | bytes 18440 | tf_op jit(solution)/shard_map/ppermute | solution.py:366
